TPU v7x, 512 devices: a whole 4x4x16 slice. The times are simulated.
512 devices in a mesh: gx: 32 (over z_lo, y), gy: 8 (over x, core), gz: 2 (over z_hi).
Axes of the slice: x: 4, y: 4, z: 16 (z_hi: 2, z_lo: 8; z = z_hi * 8 + z_lo), core: 2. Of those that a mesh axis runs over, the one named last changes fastest.
Arguments:
- features: bfloat16 [32, 8, 2, 128, 256], P('gx', 'gy', 'gz'), may hold values from -6 to 6
- positions: bfloat16 [32, 8, 2, 3, 128], P('gx', 'gy', 'gz'), may hold values from 0 to 8
- neighbours: int32 [32, 8, 2, 12, 128], P('gx', 'gy', 'gz'), may hold values from 0 to 3455
- counts: int32 [32, 8, 2, 128], P('gx', 'gy', 'gz'), may hold values from 3 to 12
- cell_index: int32 [32, 8, 2, 3, 64, 128], P('gx', 'gy', 'gz'), may hold values from 0 to 133, as said below
- spline_weight: float32 [32, 8, 2, 64, 128], P('gx', 'gy', 'gz'), may hold values from 0 to 1
- spline_slope: float32 [32, 8, 2, 3, 64, 128], P('gx', 'gy', 'gz'), may hold values from -4 to 4
- radial_in: float32 [8, 64], replicated, may hold values from -4 to 4
- radial_out: float32 [64, 192], replicated, may hold values from -0.75 to 0.75
- mix_scalar: bfloat16 [64, 64], replicated, may hold values from -1.5 to 1.5
- mix_vector: bfloat16 [64, 64], replicated, may hold values from -1.5 to 1.5
- mix_gate: bfloat16 [64, 64], replicated, may hold values from -1.5 to 1.5
- charge_head: float32 [64], replicated, may hold values from -0.75 to 0.75
Outputs:
- updated: bfloat16 [32, 8, 2, 128, 256], P('gx', 'gy', 'gz')
- forces: float32 [32, 8, 2, 3, 128], P('gx', 'gy', 'gz')
Inputs may be any that keep to these rules, and one draw needn't show every extreme that they name: `cell_index`: coordinate 0 lies below 8 + 6, coordinate 1 below 32 + 6, coordinate 2 below 128 + 6.
All inputs are finite; a program needn't handle non-finite values.
Results may differ from a plain program's by a relative error of at most 0.015.
Values may be sent and summed in bfloat16 or wider, within the bound.
A program may use at most 64 MiB of HBM per device.

v0:
```python
import math

import jax
import jax.numpy as jnp
from jax import lax
from jax.sharding import PartitionSpec as P

MESH = 256


box_side = 8.0
highest = lax.Precision.HIGHEST


def with_halo(block, sides, width):
    for axis, dim in sides:
        count = lax.axis_size(axis)
        forward = [(i, i + 1) for i in range(count - 1)]
        forward.append((count - 1, 0))
        backward = [(target, source) for source, target in forward]
        low = lax.ppermute(
            lax.slice_in_dim(block, block.shape[dim] - width, None, axis=dim), axis, forward
        )
        high = lax.ppermute(lax.slice_in_dim(block, 0, width, axis=dim), axis, backward)
        block = jnp.concatenate([low, block, high], axis=dim)
    return block


def atom_layer(
    table_feat,
    table_pos,
    own_feat,
    own_pos,
    nbr_rows,
    nbr_count,
    radial_in,
    radial_out,
    mix_scalar,
    mix_vector,
    mix_gate,
    charge_head,
):
    chan_count = own_feat.shape[1] // 4
    edge_count, atom_count = nbr_rows.shape
    flat_rows = nbr_rows.reshape(-1)
    picked = (
        jnp.take(table_feat, flat_rows, axis=0)
        .astype(jnp.float32)
        .reshape(edge_count, atom_count, 4 * chan_count)
    )
    others = jnp.take(table_pos, flat_rows, axis=1).reshape(3, edge_count, atom_count)
    delta = others - own_pos[:, None, :]
    length = jnp.sqrt(jnp.sum(delta * delta, axis=0) + 1.0)
    direction = jnp.transpose(delta / length, (1, 2, 0))
    centres = 4.0 * jnp.arange(radial_in.shape[0], dtype=jnp.float32)
    basis = jnp.exp(-jnp.square(length[:, :, None] - centres) / 8.0)
    hidden = jax.nn.silu(jnp.einsum("kan,nh->kah", basis, radial_in, precision=highest))
    radial = jnp.einsum("kah,hc->kac", hidden, radial_out, precision=highest)
    radial_zero = radial[..., :chan_count]
    radial_one = radial[..., chan_count : 2 * chan_count]
    radial_two = radial[..., 2 * chan_count :]
    scalars = picked[..., :chan_count]
    vectors = picked[..., chan_count:].reshape(edge_count, atom_count, 3, chan_count)
    along = jnp.sum(direction[..., None] * vectors, axis=2)
    live = (jnp.arange(edge_count, dtype=jnp.int32)[:, None] < nbr_count[None, :]).astype(
        jnp.float32
    )[..., None]
    message_s = (radial_zero * scalars + radial_two * along) * live
    message_v = (
        (radial_one * scalars)[:, :, None, :] * direction[..., None]
        + radial_two[:, :, None, :] * vectors
    ) * live[:, :, None, :]
    agg_s = (jnp.sum(message_s, axis=0) / edge_count).astype(jnp.bfloat16)
    agg_v = (jnp.sum(message_v, axis=0) / edge_count).astype(jnp.bfloat16)
    mixed_s = jnp.dot(agg_s, mix_scalar, preferred_element_type=jnp.float32)
    gating = jax.nn.sigmoid(jnp.dot(agg_s, mix_gate, preferred_element_type=jnp.float32))
    mixed_v = jnp.dot(
        agg_v.reshape(atom_count * 3, chan_count), mix_vector, preferred_element_type=jnp.float32
    ).reshape(atom_count, 3, chan_count)
    own_values = own_feat.astype(jnp.float32)
    new_s = own_values[:, :chan_count] + jax.nn.silu(mixed_s)
    new_v = (
        own_values[:, chan_count:].reshape(atom_count, 3, chan_count) + mixed_v * gating[:, None, :]
    )
    result = jnp.concatenate([new_s, new_v.reshape(atom_count, 3 * chan_count)], axis=1).astype(
        jnp.bfloat16
    )
    charge = jnp.dot(result[:, :chan_count].astype(jnp.float32), charge_head, precision=highest)
    return (result, charge)


def green_values(freq_x, freq_y, freq_z, mesh_cells):

    def signed(index):
        return jnp.where(2 * index < mesh_cells, index, index - mesh_cells).astype(jnp.float32)

    step_size = 2.0 * math.pi / mesh_cells
    ksquare = (
        step_size
        * step_size
        * (jnp.square(signed(freq_x)) + jnp.square(signed(freq_y)) + jnp.square(signed(freq_z)))
    )
    screen = 4.0 * math.pi / mesh_cells
    value = jnp.exp(-0.5 * ksquare) / (ksquare + screen * screen)
    anchor = (freq_x == 0) & (freq_y == 0) & (freq_z == 0)
    return jnp.where(anchor, jnp.zeros_like(value), value)


def dft_tables(mesh_cells):
    series = jnp.arange(mesh_cells, dtype=jnp.int32)
    product = series[:, None] * series[None, :] % mesh_cells
    angle = product.astype(jnp.float32) * (2.0 * math.pi / mesh_cells)
    return (jnp.cos(angle), jnp.sin(angle))


def transform(real_part, imag_part, cosine_table, sine_table, pattern, orient):
    new_real = jnp.einsum(
        pattern, real_part, cosine_table, precision=highest
    ) - orient * jnp.einsum(pattern, imag_part, sine_table, precision=highest)
    new_imag = jnp.einsum(
        pattern, imag_part, cosine_table, precision=highest
    ) + orient * jnp.einsum(pattern, real_part, sine_table, precision=highest)
    return (new_real, new_imag)


def fold_rims(extended, which, core):
    middle = lax.slice_in_dim(extended, 6, 6 + core, axis=which)
    lower = lax.slice_in_dim(extended, 0, 3, axis=which)
    upper = lax.slice_in_dim(extended, core + 9, core + 12, axis=which)
    low_width = [(0, 0)] * extended.ndim
    low_width[which] = (0, core - 3)
    high_width = [(0, 0)] * extended.ndim
    high_width[which] = (core - 3, 0)
    return middle + jnp.pad(lower, low_width) + jnp.pad(upper, high_width)


def per_device(
    features,
    positions,
    neighbours,
    counts,
    cell_index,
    spline_weight,
    spline_slope,
    radial_in,
    radial_out,
    mix_scalar,
    mix_vector,
    mix_gate,
    charge_head,
):
    ghost_feat, ghost_pos = (
        with_halo(features, (("gx", 0), ("gy", 1), ("gz", 2)), 1),
        with_halo(positions, (("gx", 0), ("gy", 1), ("gz", 2)), 1),
    )
    atom_count = features.shape[3]
    shifts = (jnp.arange(3, dtype=jnp.float32) - 1.0) * box_side
    offsets = jnp.stack(
        [
            jnp.broadcast_to(shifts[:, None, None], (3, 3, 3)),
            jnp.broadcast_to(shifts[None, :, None], (3, 3, 3)),
            jnp.broadcast_to(shifts[None, None, :], (3, 3, 3)),
        ],
        axis=-1,
    )
    table_pos = ghost_pos.astype(jnp.float32) + offsets[..., None]
    table_pos = jnp.moveaxis(table_pos, 3, 0).reshape(3, 27 * atom_count)
    table_feat = ghost_feat.reshape(27 * atom_count, features.shape[4])
    updated, charge = atom_layer(
        table_feat,
        table_pos,
        features[0, 0, 0],
        positions[0, 0, 0].astype(jnp.float32),
        neighbours[0, 0, 0],
        counts[0, 0, 0],
        radial_in,
        radial_out,
        mix_scalar,
        mix_vector,
        mix_gate,
        charge_head,
    )
    wide_x, wide_y, wide_z = (lax.axis_size("gx"), lax.axis_size("gy"), lax.axis_size("gz"))
    block_x, block_y, block_z = (MESH // wide_x, MESH // wide_y, MESH // wide_z)
    padded_shape = (block_x + 6, block_y + 6, block_z + 6)
    coords = cell_index[0, 0, 0]
    flat_cells = (coords[0] * padded_shape[1] + coords[1]) * padded_shape[2] + coords[2]
    local_cells = flat_cells.reshape(-1)
    spread = (charge[None, :] * spline_weight[0, 0, 0]).reshape(-1)
    density = (
        jnp.zeros((padded_shape[0] * padded_shape[1] * padded_shape[2],), jnp.float32)
        .at[local_cells]
        .add(spread)
        .reshape(padded_shape)
    )
    extended = with_halo(density, (("gx", 0), ("gy", 1), ("gz", 2)), 3)
    extended = fold_rims(extended, 0, block_x)
    extended = fold_rims(extended, 1, block_y)
    owned = fold_rims(extended, 2, block_z)
    cosine_table, sine_table = dft_tables(MESH)
    column = lax.all_gather(owned, "gz", axis=2, tiled=True)
    group = lax.axis_index("gx")
    span_y = MESH // wide_x
    real_part = jnp.einsum("xyz,zk->xyk", column, cosine_table, precision=highest)
    imag_part = -jnp.einsum("xyz,zk->xyk", column, sine_table, precision=highest)
    real_part, imag_part = (
        lax.all_to_all(
            real_part.astype(jnp.bfloat16), "gy", split_axis=2, concat_axis=1, tiled=True
        ).astype(real_part.dtype),
        lax.all_to_all(
            imag_part.astype(jnp.bfloat16), "gy", split_axis=2, concat_axis=1, tiled=True
        ).astype(imag_part.dtype),
    )
    span_z = MESH // wide_y
    real_part, imag_part = transform(
        real_part, imag_part, cosine_table, sine_table, "xyz,yk->xkz", -1.0
    )
    real_part, imag_part = (
        lax.all_to_all(
            real_part.astype(jnp.bfloat16), "gx", split_axis=1, concat_axis=0, tiled=True
        ).astype(real_part.dtype),
        lax.all_to_all(
            imag_part.astype(jnp.bfloat16), "gx", split_axis=1, concat_axis=0, tiled=True
        ).astype(imag_part.dtype),
    )
    real_part, imag_part = transform(
        real_part, imag_part, cosine_table, sine_table, "xyz,xk->kyz", -1.0
    )
    freq_z = lax.axis_index("gy") * span_z + jnp.arange(span_z, dtype=jnp.int32)
    slot_range = group * span_y + jnp.arange(span_y, dtype=jnp.int32)
    freq_x = jnp.arange(MESH, dtype=jnp.int32)[:, None, None]
    green = green_values(freq_x, slot_range[None, :, None], freq_z[None, None, :], MESH)
    real_part, imag_part = (real_part * green, imag_part * green)
    real_part, imag_part = transform(
        real_part, imag_part, cosine_table, sine_table, "xyz,xk->kyz", 1.0
    )
    real_part, imag_part = (
        lax.all_to_all(
            real_part.astype(jnp.bfloat16), "gx", split_axis=0, concat_axis=1, tiled=True
        ).astype(real_part.dtype),
        lax.all_to_all(
            imag_part.astype(jnp.bfloat16), "gx", split_axis=0, concat_axis=1, tiled=True
        ).astype(imag_part.dtype),
    )
    real_part, imag_part = transform(
        real_part, imag_part, cosine_table, sine_table, "xyz,yk->xkz", 1.0
    )
    real_part, imag_part = (
        lax.all_to_all(
            real_part.astype(jnp.bfloat16), "gy", split_axis=1, concat_axis=2, tiled=True
        ).astype(real_part.dtype),
        lax.all_to_all(
            imag_part.astype(jnp.bfloat16), "gy", split_axis=1, concat_axis=2, tiled=True
        ).astype(imag_part.dtype),
    )
    potential = (
        jnp.einsum("xyz,zk->xyk", real_part, cosine_table, precision=highest)
        - jnp.einsum("xyz,zk->xyk", imag_part, sine_table, precision=highest)
    ) / float(MESH) ** 3
    owned_potential = lax.dynamic_slice_in_dim(
        potential, lax.axis_index("gz") * block_z, block_z, 2
    )
    padded_potential = with_halo(owned_potential, (("gx", 0), ("gy", 1), ("gz", 2)), 3)
    values = jnp.take(padded_potential.reshape(-1), flat_cells, axis=0)
    forces = -charge[None, :] * jnp.sum(spline_slope[0, 0, 0] * values[None, :, :], axis=1)
    return (updated[None, None, None], forces[None, None, None])


def solution(mesh):
    placed = (
        P("gx", "gy", "gz", None, None),
        P("gx", "gy", "gz", None, None),
        P("gx", "gy", "gz", None, None),
        P("gx", "gy", "gz", None),
        P("gx", "gy", "gz", None, None, None),
        P("gx", "gy", "gz", None, None),
        P("gx", "gy", "gz", None, None, None),
        P(),
        P(),
        P(),
        P(),
        P(),
        P(),
    )
    return jax.shard_map(
        per_device,
        mesh=mesh,
        in_specs=placed,
        out_specs=(P("gx", "gy", "gz", None, None), P("gx", "gy", "gz", None, None)),
        check_vma=False,
    )
```

profile of v0, /device:TPU:1, one launch (start us, length us, event | category | flops | bytes accessed | tf_op | source)
XLA Modules:
  0.0 634.5 jit_solution(7109187416329862315)
XLA Ops:
  4.8 14.0 %collective-permute-start.1 = (bf16[1,1,1,3,128]{4,3,2,1,0:T(4,128)(2,1)}, bf16[1,1,1,3,128]{4,3,2,1,0:T(4,128)(2,1)S(1)}, u32[]{:S(2)}, u32[]{:S(2)}) collective-permute-start(bf16[1,1,1,3,128]{4,3,2,1,0:T(4,128)(2,1)} %param.14), channel_id=1, source_target_pairs={{16,0},{32,16},{48,32},{64,48},{80,64},{96,80},{112,96},{128,112},... | collective-permute-start | bytes 2312 | tf_op jit(solution)/shard_map/ppermute | solution.py:24
  20.8 12.1 %collective-permute-start.7 = (bf16[1,1,1,128,256]{4,3,2,1,0:T(8,128)(2,1)}, bf16[1,1,1,128,256]{4,3,2,1,0:T(8,128)(2,1)S(1)}, u32[]{:S(2)}, u32[]{:S(2)}) collective-permute-start(bf16[1,1,1,128,256]{4,3,2,1,0:T(8,128)(2,1)} %param.13), channel_id=1, source_target_pairs={{16,0},{32,16},{48,32},{64,48},{80,64},{96,80},{112,96},{128,112},... | collective-permute-start | bytes 196616 | tf_op jit(solution)/shard_map/ppermute | solution.py:24
  46.8 11.3 %collective-permute-start.5 = (bf16[3,3,1,3,128]{4,3,2,1,0:T(4,128)(2,1)S(1)}, bf16[3,3,1,3,128]{4,3,2,1,0:T(4,128)(2,1)S(1)}, u32[]{:S(2)}, u32[]{:S(2)}) collective-permute-start(bf16[3,3,1,3,128]{4,3,2,1,0:T(4,128)(2,1)S(1)} %pad_maximum_fusion.11), channel_id=1, source_target_pairs={{1,0},{0,1},{3,2},{2,3},{5,4},{4,5},{7,6},{6,7},{9,8},{8,9},{11,10... | collective-permute-start | bytes 20744 | tf_op jit(solution)/shard_map/ppermute | solution.py:24
  61.4 9.8 %collective-permute-done.4 = bf16[3,3,1,3,128]{4,3,2,1,0:T(4,128)(2,1)S(1)} collective-permute-done((bf16[3,3,1,3,128]{4,3,2,1,0:T(4,128)(2,1)S(1)}, bf16[3,3,1,3,128]{4,3,2,1,0:T(4,128)(2,1)S(1)}, u32[]{:S(2)}, u32[]{:S(2)}) %collective-permute-start.4) | collective-permute-done | bytes 6944 | tf_op jit(solution)/shard_map/ppermute | solution.py:21
  75.0 4.4 collective-permute-start.9
  85.0 11.1 %collective-permute-start.10 = (bf16[3,3,1,128,256]{4,3,2,1,0:T(8,128)(2,1)S(1)}, bf16[3,3,1,128,256]{4,3,2,1,0:T(8,128)(2,1)}, u32[]{:S(2)}, u32[]{:S(2)}) collective-permute-start(bf16[3,3,1,128,256]{4,3,2,1,0:T(8,128)(2,1)S(1)} %pad_maximum_fusion.3), channel_id=1, source_target_pairs={{0,1},{1,0},{2,3},{3,2},{4,5},{5,4},{6,7},{7,6},{8,9},{9,8},{10,11... | collective-permute-start | bytes 1769480 | tf_op jit(solution)/shard_map/ppermute | solution.py:21
  100.4 69.2 %collective-permute-done.11 = bf16[3,3,1,128,256]{4,3,2,1,0:T(8,128)(2,1)S(1)} collective-permute-done((bf16[3,3,1,128,256]{4,3,2,1,0:T(8,128)(2,1)S(1)}, bf16[3,3,1,128,256]{4,3,2,1,0:T(8,128)(2,1)S(1)}, u32[]{:S(2)}, u32[]{:S(2)}) %collective-permute-start.11) | collective-permute-done | bytes 589856 | tf_op jit(solution)/shard_map/ppermute | solution.py:24
  170.4 11.9 %collective-permute-done.10 = bf16[3,3,1,128,256]{4,3,2,1,0:T(8,128)(2,1)} collective-permute-done((bf16[3,3,1,128,256]{4,3,2,1,0:T(8,128)(2,1)S(1)}, bf16[3,3,1,128,256]{4,3,2,1,0:T(8,128)(2,1)}, u32[]{:S(2)}, u32[]{:S(2)}) %collective-permute-start.10) | collective-permute-done | bytes 589856 | tf_op jit(solution)/shard_map/ppermute | solution.py:21
  183.8 4.8 gather_fusion.1
  192.7 43.4 %scatter_custom_fusion = f32[71288]{0:T(1024)S(1)} fusion(s32[8192]{0:T(1024)} %bitcast.301, f32[8192]{0:T(1024)S(1)} %bitcast_multiply_fusion.2, f32[]{:T(128)} %constant.58.clone.1), kind=kCustom, calls=%fused_computation.95 | custom fusion | flops 8192 | bytes 285664 | tf_op jit(solution)/shard_map/scatter-add | solution.py:193
  239.7 12.1 %collective-permute-start.13 = (f32[3,38,134]{2,1,0:T(8,128)S(1)}, f32[3,38,134]{2,1,0:T(8,128)S(1)}, u32[]{:S(2)}, u32[]{:S(2)}) collective-permute-start(f32[3,38,134]{2,1,0:T(8,128)S(1)} %slice.135), channel_id=1, source_target_pairs={{16,0},{32,16},{48,32},{64,48},{80,64},{96,80},{112,96},{128,112},... | collective-permute-start | bytes 183320 | tf_op jit(solution)/shard_map/ppermute | solution.py:24
  261.6 8.7 %collective-permute-start.16 = (f32[20,44,3]{2,1,0:T(8,128)}, f32[20,44,3]{2,1,0:T(8,128)S(1)}, u32[]{:S(2)}, u32[]{:S(2)}) collective-permute-start(f32[20,44,3]{2,1,0:T(8,128)} %get-tuple-element.7), channel_id=1, source_target_pairs={{0,1},{1,0},{2,3},{3,2},{4,5},{5,4},{6,7},{7,6},{8,9},{9,8},{10,11... | collective-permute-start | bytes 31688 | tf_op jit(solution)/shard_map/ppermute | solution.py:21
  270.3 5.3 collective-permute-start.17
  276.1 21.3 %collective-permute-done.16 = f32[20,44,3]{2,1,0:T(8,128)S(1)} collective-permute-done((f32[20,44,3]{2,1,0:T(8,128)}, f32[20,44,3]{2,1,0:T(8,128)S(1)}, u32[]{:S(2)}, u32[]{:S(2)}) %collective-permute-start.16) | collective-permute-done | bytes 10592 | tf_op jit(solution)/shard_map/ppermute | solution.py:21
  297.4 10.7 %collective-permute-done.17 = f32[20,44,3]{2,1,0:T(8,128)S(1)} collective-permute-done((f32[20,44,3]{2,1,0:T(8,128)}, f32[20,44,3]{2,1,0:T(8,128)S(1)}, u32[]{:S(2)}, u32[]{:S(2)}) %collective-permute-start.17) | collective-permute-done | bytes 10592 | tf_op jit(solution)/shard_map/ppermute | solution.py:24
  310.5 51.6 %all_gather.3 = f32[8,32,256]{2,1,0:T(8,128)S(1)} all-gather(f32[8,32,128]{2,1,0:T(8,128)S(1)} %fusion.54), channel_id=1, replica_groups=mesh['gx'=32,'gy'=8,'gz'=2] {'gz'}, dimensions={2}, use_global_device_ids=true | all-gather | bytes 393216 | tf_op jit(solution)/shard_map/all_gather | solution.py:201
  365.0 4.9 all-to-all-start
  388.4 16.3 %all-to-all-start.2 = ((bf16[32,2,1024]{2,1,0:T(2,128)(2,1)}), bf16[32,2,1024]{2,1,0:T(2,128)(2,1)S(1)}, u32[]{:S(2)}, u32[]{:S(2)}) async-start(bf16[32,2,1024]{2,1,0:T(2,128)(2,1)} %reshape.633), calls=%async_computation.2 | async-start | bytes 262144 | tf_op jit(solution)/shard_map/all_to_all | solution.py:219
  408.8 8.0 %all-to-all-done.2 = bf16[32,2,1024]{2,1,0:T(2,128)(2,1)S(1)} async-done(((bf16[32,2,1024]{2,1,0:T(2,128)(2,1)}), bf16[32,2,1024]{2,1,0:T(2,128)(2,1)S(1)}, u32[]{:S(2)}, u32[]{:S(2)}) %all-to-all-start.2) | async-done | bytes 131104 | tf_op jit(solution)/shard_map/all_to_all | solution.py:219
  416.8 7.1 %all-to-all-start.3 = ((bf16[32,2,1024]{2,1,0:T(2,128)(2,1)}), bf16[32,2,1024]{2,1,0:T(2,128)(2,1)S(1)}, u32[]{:S(2)}, u32[]{:S(2)}) async-start(bf16[32,2,1024]{2,1,0:T(2,128)(2,1)} %reshape.631), calls=%async_computation.3 | async-start | bytes 262144 | tf_op jit(solution)/shard_map/all_to_all | solution.py:222
  427.7 8.4 %all-to-all-done.3 = bf16[32,2,1024]{2,1,0:T(2,128)(2,1)S(1)} async-done(((bf16[32,2,1024]{2,1,0:T(2,128)(2,1)}), bf16[32,2,1024]{2,1,0:T(2,128)(2,1)S(1)}, u32[]{:S(2)}, u32[]{:S(2)}) %all-to-all-start.3) | async-done | bytes 131104 | tf_op jit(solution)/shard_map/all_to_all | solution.py:222
  443.9 6.6 %all-to-all-start.5 = ((bf16[32,2,1024]{2,1,0:T(2,128)(2,1)}), bf16[32,2,1024]{2,1,0:T(2,128)(2,1)S(1)}, u32[]{:S(2)}, u32[]{:S(2)}) async-start(bf16[32,2,1024]{2,1,0:T(2,128)(2,1)} %reshape.635), calls=%async_computation.5 | async-start | bytes 262144 | tf_op jit(solution)/shard_map/all_to_all | solution.py:241
  454.7 7.8 %all-to-all-done.5 = bf16[32,2,1024]{2,1,0:T(2,128)(2,1)S(1)} async-done(((bf16[32,2,1024]{2,1,0:T(2,128)(2,1)}), bf16[32,2,1024]{2,1,0:T(2,128)(2,1)S(1)}, u32[]{:S(2)}, u32[]{:S(2)}) %all-to-all-start.5) | async-done | bytes 131104 | tf_op jit(solution)/shard_map/all_to_all | solution.py:241
  462.5 6.3 all-to-all-start.4
  471.9 9.0 %all-to-all-done.4 = bf16[32,2,1024]{2,1,0:T(2,128)(2,1)S(1)} async-done(((bf16[32,2,1024]{2,1,0:T(2,128)(2,1)}), bf16[32,2,1024]{2,1,0:T(2,128)(2,1)S(1)}, u32[]{:S(2)}, u32[]{:S(2)}) %all-to-all-start.4) | async-done | bytes 131104 | tf_op jit(solution)/shard_map/all_to_all | solution.py:238
  485.6 6.3 all-to-all-start.6
  511.5 11.7 %collective-permute-start.19 = (f32[3,32,128]{2,1,0:T(8,128)S(1)}, f32[3,32,128]{2,1,0:T(8,128)S(1)}, u32[]{:S(2)}, u32[]{:S(2)}) collective-permute-start(f32[3,32,128]{2,1,0:T(8,128)S(1)} %get-tuple-element.18), channel_id=1, source_target_pairs={{16,0},{32,16},{48,32},{64,48},{80,64},{96,80},{112,96},{128,112},... | collective-permute-start | bytes 147464 | tf_op jit(solution)/shard_map/ppermute | solution.py:24
  530.3 8.8 %collective-permute-start.22 = (f32[14,38,3]{2,1,0:T(8,128)S(1)}, f32[14,38,3]{2,1,0:T(8,128)S(1)}, u32[]{:S(2)}, u32[]{:S(2)}) collective-permute-start(f32[14,38,3]{2,1,0:T(8,128)S(1)} %get-tuple-element.11), channel_id=1, source_target_pairs={{0,1},{1,0},{2,3},{3,2},{4,5},{5,4},{6,7},{7,6},{8,9},{9,8},{10,11... | collective-permute-start | bytes 19160 | tf_op jit(solution)/shard_map/ppermute | solution.py:21
  539.1 5.2 collective-permute-start.23
  545.0 36.1 %collective-permute-done.22 = f32[14,38,3]{2,1,0:T(8,128)S(1)} collective-permute-done((f32[14,38,3]{2,1,0:T(8,128)S(1)}, f32[14,38,3]{2,1,0:T(8,128)S(1)}, u32[]{:S(2)}, u32[]{:S(2)}) %collective-permute-start.22) | collective-permute-done | bytes 6416 | tf_op jit(solution)/shard_map/ppermute | solution.py:21
  581.1 6.3 collective-permute-done.23
  588.1 45.5 %gather_fusion.2 = f32[8192]{0:T(1024)S(1)} fusion(f32[71288]{0:T(1024)S(1)} %reshape.549, s32[8192]{0:T(1024)S(1)} %copy-done.13), kind=kCustom, calls=%fused_computation.2 | custom fusion | bytes 98304 | tf_op jit(solution)/shard_map/jit(_take)/gather | solution.py:264
  (265 shorter events, 136.6 us)
Async XLA Ops:
  0.6 40.3 %collective-permute-start = (bf16[1,1,1,3,128]{4,3,2,1,0:T(4,128)(2,1)}, bf16[1,1,1,3,128]{4,3,2,1,0:T(4,128)(2,1)S(1)}, u32[]{:S(2)}, u32[]{:S(2)}) collective-permute-start(bf16[1,1,1,3,128]{4,3,2,1,0:T(4,128)(2,1)} %param.14), channel_id=1, source_target_pairs={{0,16},{16,32},{32,48},{48,64},{64,80},{80,96},{96,112},{112,128},... | collective-permute-start | bytes 2312 | tf_op jit(solution)/shard_map/ppermute | solution.py:21
  4.8 36.8 %collective-permute-start.1 = (bf16[1,1,1,3,128]{4,3,2,1,0:T(4,128)(2,1)}, bf16[1,1,1,3,128]{4,3,2,1,0:T(4,128)(2,1)S(1)}, u32[]{:S(2)}, u32[]{:S(2)}) collective-permute-start(bf16[1,1,1,3,128]{4,3,2,1,0:T(4,128)(2,1)} %param.14), channel_id=1, source_target_pairs={{16,0},{32,16},{48,32},{64,48},{80,64},{96,80},{112,96},{128,112},... | collective-permute-start | bytes 2312 | tf_op jit(solution)/shard_map/ppermute | solution.py:24
  18.9 56.1 %collective-permute-start.6 = (bf16[1,1,1,128,256]{4,3,2,1,0:T(8,128)(2,1)}, bf16[1,1,1,128,256]{4,3,2,1,0:T(8,128)(2,1)S(1)}, u32[]{:S(2)}, u32[]{:S(2)}) collective-permute-start(bf16[1,1,1,128,256]{4,3,2,1,0:T(8,128)(2,1)} %param.13), channel_id=1, source_target_pairs={{0,16},{16,32},{32,48},{48,64},{64,80},{80,96},{96,112},{112,128},... | collective-permute-start | bytes 196616 | tf_op jit(solution)/shard_map/ppermute | solution.py:21
  20.8 54.2 %collective-permute-start.7 = (bf16[1,1,1,128,256]{4,3,2,1,0:T(8,128)(2,1)}, bf16[1,1,1,128,256]{4,3,2,1,0:T(8,128)(2,1)S(1)}, u32[]{:S(2)}, u32[]{:S(2)}) collective-permute-start(bf16[1,1,1,128,256]{4,3,2,1,0:T(8,128)(2,1)} %param.13), channel_id=1, source_target_pairs={{16,0},{32,16},{48,32},{64,48},{80,64},{96,80},{112,96},{128,112},... | collective-permute-start | bytes 196616 | tf_op jit(solution)/shard_map/ppermute | solution.py:24
  41.7 4.7 collective-permute-start.3
  45.6 1.2 collective-permute-start.2
  46.8 14.6 %collective-permute-start.5 = (bf16[3,3,1,3,128]{4,3,2,1,0:T(4,128)(2,1)S(1)}, bf16[3,3,1,3,128]{4,3,2,1,0:T(4,128)(2,1)S(1)}, u32[]{:S(2)}, u32[]{:S(2)}) collective-permute-start(bf16[3,3,1,3,128]{4,3,2,1,0:T(4,128)(2,1)S(1)} %pad_maximum_fusion.11), channel_id=1, source_target_pairs={{1,0},{0,1},{3,2},{2,3},{5,4},{4,5},{7,6},{6,7},{9,8},{8,9},{11,10... | collective-permute-start | bytes 20744 | tf_op jit(solution)/shard_map/ppermute | solution.py:24
  58.1 13.1 %collective-permute-start.4 = (bf16[3,3,1,3,128]{4,3,2,1,0:T(4,128)(2,1)S(1)}, bf16[3,3,1,3,128]{4,3,2,1,0:T(4,128)(2,1)S(1)}, u32[]{:S(2)}, u32[]{:S(2)}) collective-permute-start(bf16[3,3,1,3,128]{4,3,2,1,0:T(4,128)(2,1)S(1)} %pad_maximum_fusion.11), channel_id=1, source_target_pairs={{0,1},{1,0},{2,3},{3,2},{4,5},{5,4},{6,7},{7,6},{8,9},{9,8},{10,11... | collective-permute-start | bytes 20744 | tf_op jit(solution)/shard_map/ppermute | solution.py:21
  75.0 6.6 %collective-permute-start.9 = (bf16[3,1,1,128,256]{4,3,2,1,0:T(8,128)(2,1)S(1)}, bf16[3,1,1,128,256]{4,3,2,1,0:T(8,128)(2,1)S(1)}, u32[]{:S(2)}, u32[]{:S(2)}) collective-permute-start(bf16[3,1,1,128,256]{4,3,2,1,0:T(8,128)(2,1)S(1)} %constant_dynamic-update-slice_fusion.3), channel_id=1, source_target_pairs={{2,0},{4,2},{6,4},{8,6},{10,8},{12,10},{14,12},{0,14},{3,1},{5,3},... | collective-permute-start | bytes 589832 | tf_op jit(solution)/shard_map/ppermute | solution.py:24
  79.4 2.6 collective-permute-start.8
  82.1 87.5 %collective-permute-start.11 = (bf16[3,3,1,128,256]{4,3,2,1,0:T(8,128)(2,1)S(1)}, bf16[3,3,1,128,256]{4,3,2,1,0:T(8,128)(2,1)S(1)}, u32[]{:S(2)}, u32[]{:S(2)}) collective-permute-start(bf16[3,3,1,128,256]{4,3,2,1,0:T(8,128)(2,1)S(1)} %pad_maximum_fusion.3), channel_id=1, source_target_pairs={{1,0},{0,1},{3,2},{2,3},{5,4},{4,5},{7,6},{6,7},{9,8},{8,9},{11,10... | collective-permute-start | bytes 1769480 | tf_op jit(solution)/shard_map/ppermute | solution.py:24
  85.0 97.4 %collective-permute-start.10 = (bf16[3,3,1,128,256]{4,3,2,1,0:T(8,128)(2,1)S(1)}, bf16[3,3,1,128,256]{4,3,2,1,0:T(8,128)(2,1)}, u32[]{:S(2)}, u32[]{:S(2)}) collective-permute-start(bf16[3,3,1,128,256]{4,3,2,1,0:T(8,128)(2,1)S(1)} %pad_maximum_fusion.3), channel_id=1, source_target_pairs={{0,1},{1,0},{2,3},{3,2},{4,5},{5,4},{6,7},{7,6},{8,9},{9,8},{10,11... | collective-permute-start | bytes 1769480 | tf_op jit(solution)/shard_map/ppermute | solution.py:21
  236.4 15.3 %collective-permute-start.12 = (f32[3,38,134]{2,1,0:T(8,128)S(1)}, f32[3,38,134]{2,1,0:T(8,128)S(1)}, u32[]{:S(2)}, u32[]{:S(2)}) collective-permute-start(f32[3,38,134]{2,1,0:T(8,128)S(1)} %slice.133), channel_id=1, source_target_pairs={{0,16},{16,32},{32,48},{48,64},{64,80},{80,96},{96,112},{112,128},... | collective-permute-start | bytes 183320 | tf_op jit(solution)/shard_map/ppermute | solution.py:21
  239.7 13.9 %collective-permute-start.13 = (f32[3,38,134]{2,1,0:T(8,128)S(1)}, f32[3,38,134]{2,1,0:T(8,128)S(1)}, u32[]{:S(2)}, u32[]{:S(2)}) collective-permute-start(f32[3,38,134]{2,1,0:T(8,128)S(1)} %slice.135), channel_id=1, source_target_pairs={{16,0},{32,16},{48,32},{64,48},{80,64},{96,80},{112,96},{128,112},... | collective-permute-start | bytes 183320 | tf_op jit(solution)/shard_map/ppermute | solution.py:24
  253.7 4.3 collective-permute-start.14
  256.5 3.9 collective-permute-start.15
  261.6 35.8 %collective-permute-start.16 = (f32[20,44,3]{2,1,0:T(8,128)}, f32[20,44,3]{2,1,0:T(8,128)S(1)}, u32[]{:S(2)}, u32[]{:S(2)}) collective-permute-start(f32[20,44,3]{2,1,0:T(8,128)} %get-tuple-element.7), channel_id=1, source_target_pairs={{0,1},{1,0},{2,3},{3,2},{4,5},{5,4},{6,7},{7,6},{8,9},{9,8},{10,11... | collective-permute-start | bytes 31688 | tf_op jit(solution)/shard_map/ppermute | solution.py:21
  270.3 37.8 %collective-permute-start.17 = (f32[20,44,3]{2,1,0:T(8,128)}, f32[20,44,3]{2,1,0:T(8,128)S(1)}, u32[]{:S(2)}, u32[]{:S(2)}) collective-permute-start(f32[20,44,3]{2,1,0:T(8,128)} %get-tuple-element.8), channel_id=1, source_target_pairs={{1,0},{0,1},{3,2},{2,3},{5,4},{4,5},{7,6},{6,7},{9,8},{8,9},{11,10... | collective-permute-start | bytes 31688 | tf_op jit(solution)/shard_map/ppermute | solution.py:24
  365.0 10.2 %all-to-all-start = ((bf16[8,2,4096]{2,1,0:T(2,128)(2,1)}), bf16[8,2,4096]{2,1,0:T(2,128)(2,1)S(1)}, u32[]{:S(2)}, u32[]{:S(2)}) async-start(bf16[8,2,4096]{2,1,0:T(2,128)(2,1)} %reshape.629), calls=%async_computation | async-start | bytes 262144 | tf_op jit(solution)/shard_map/all_to_all | solution.py:207
  375.2 9.4 %all-to-all-start.1 = ((bf16[8,2,4096]{2,1,0:T(2,128)(2,1)}), bf16[8,2,4096]{2,1,0:T(2,128)(2,1)S(1)}, u32[]{:S(2)}, u32[]{:S(2)}) async-start(bf16[8,2,4096]{2,1,0:T(2,128)(2,1)} %reshape.627), calls=%async_computation.1 | async-start | bytes 262144 | tf_op jit(solution)/shard_map/all_to_all | solution.py:210
  388.4 28.4 %all-to-all-start.2 = ((bf16[32,2,1024]{2,1,0:T(2,128)(2,1)}), bf16[32,2,1024]{2,1,0:T(2,128)(2,1)S(1)}, u32[]{:S(2)}, u32[]{:S(2)}) async-start(bf16[32,2,1024]{2,1,0:T(2,128)(2,1)} %reshape.633), calls=%async_computation.2 | async-start | bytes 262144 | tf_op jit(solution)/shard_map/all_to_all | solution.py:219
  416.8 19.2 %all-to-all-start.3 = ((bf16[32,2,1024]{2,1,0:T(2,128)(2,1)}), bf16[32,2,1024]{2,1,0:T(2,128)(2,1)S(1)}, u32[]{:S(2)}, u32[]{:S(2)}) async-start(bf16[32,2,1024]{2,1,0:T(2,128)(2,1)} %reshape.631), calls=%async_computation.3 | async-start | bytes 262144 | tf_op jit(solution)/shard_map/all_to_all | solution.py:222
  443.9 18.7 %all-to-all-start.5 = ((bf16[32,2,1024]{2,1,0:T(2,128)(2,1)}), bf16[32,2,1024]{2,1,0:T(2,128)(2,1)S(1)}, u32[]{:S(2)}, u32[]{:S(2)}) async-start(bf16[32,2,1024]{2,1,0:T(2,128)(2,1)} %reshape.635), calls=%async_computation.5 | async-start | bytes 262144 | tf_op jit(solution)/shard_map/all_to_all | solution.py:241
  462.5 18.4 %all-to-all-start.4 = ((bf16[32,2,1024]{2,1,0:T(2,128)(2,1)}), bf16[32,2,1024]{2,1,0:T(2,128)(2,1)S(1)}, u32[]{:S(2)}, u32[]{:S(2)}) async-start(bf16[32,2,1024]{2,1,0:T(2,128)(2,1)} %reshape.637), calls=%async_computation.4 | async-start | bytes 262144 | tf_op jit(solution)/shard_map/all_to_all | solution.py:238
  485.6 11.6 %all-to-all-start.6 = ((bf16[8,2,4096]{2,1,0:T(2,128)(2,1)}), bf16[8,2,4096]{2,1,0:T(2,128)(2,1)S(1)}, u32[]{:S(2)}, u32[]{:S(2)}) async-start(bf16[8,2,4096]{2,1,0:T(2,128)(2,1)} %reshape.641), calls=%async_computation.6 | async-start | bytes 262144 | tf_op jit(solution)/shard_map/all_to_all | solution.py:249
  497.1 9.6 %all-to-all-start.7 = ((bf16[8,2,4096]{2,1,0:T(2,128)(2,1)}), bf16[8,2,4096]{2,1,0:T(2,128)(2,1)S(1)}, u32[]{:S(2)}, u32[]{:S(2)}) async-start(bf16[8,2,4096]{2,1,0:T(2,128)(2,1)} %reshape.639), calls=%async_computation.7 | async-start | bytes 262144 | tf_op jit(solution)/shard_map/all_to_all | solution.py:252
  509.2 14.2 %collective-permute-start.18 = (f32[3,32,128]{2,1,0:T(8,128)S(1)}, f32[3,32,128]{2,1,0:T(8,128)S(1)}, u32[]{:S(2)}, u32[]{:S(2)}) collective-permute-start(f32[3,32,128]{2,1,0:T(8,128)S(1)} %get-tuple-element.17), channel_id=1, source_target_pairs={{0,16},{16,32},{32,48},{48,64},{64,80},{80,96},{96,112},{112,128},... | collective-permute-start | bytes 147464 | tf_op jit(solution)/shard_map/ppermute | solution.py:21
  511.5 12.8 %collective-permute-start.19 = (f32[3,32,128]{2,1,0:T(8,128)S(1)}, f32[3,32,128]{2,1,0:T(8,128)S(1)}, u32[]{:S(2)}, u32[]{:S(2)}) collective-permute-start(f32[3,32,128]{2,1,0:T(8,128)S(1)} %get-tuple-element.18), channel_id=1, source_target_pairs={{16,0},{32,16},{48,32},{64,48},{80,64},{96,80},{112,96},{128,112},... | collective-permute-start | bytes 147464 | tf_op jit(solution)/shard_map/ppermute | solution.py:24
  524.3 3.2 collective-permute-start.20
  526.5 3.6 collective-permute-start.21
  530.3 50.8 %collective-permute-start.22 = (f32[14,38,3]{2,1,0:T(8,128)S(1)}, f32[14,38,3]{2,1,0:T(8,128)S(1)}, u32[]{:S(2)}, u32[]{:S(2)}) collective-permute-start(f32[14,38,3]{2,1,0:T(8,128)S(1)} %get-tuple-element.11), channel_id=1, source_target_pairs={{0,1},{1,0},{2,3},{3,2},{4,5},{5,4},{6,7},{7,6},{8,9},{9,8},{10,11... | collective-permute-start | bytes 19160 | tf_op jit(solution)/shard_map/ppermute | solution.py:21
  539.1 48.3 %collective-permute-start.23 = (f32[14,38,3]{2,1,0:T(8,128)S(1)}, f32[14,38,3]{2,1,0:T(8,128)S(1)}, u32[]{:S(2)}, u32[]{:S(2)}) collective-permute-start(f32[14,38,3]{2,1,0:T(8,128)S(1)} %get-tuple-element.12), channel_id=1, source_target_pairs={{1,0},{0,1},{3,2},{2,3},{5,4},{4,5},{7,6},{6,7},{9,8},{8,9},{11,10... | collective-permute-start | bytes 19160 | tf_op jit(solution)/shard_map/ppermute | solution.py:24
  (39 other events, 902.9 us)
where the time goes:
time: 643 us; the launch traced here: 635 us
  waiting for transfers between devices  223 us (35%)
  starting transfers between devices  185 us (29%)
  local copies, waits for them, and re-layouts  79.3 us (12%)
  other arithmetic  62.4 us (10%)
  blocking collectives  51.6 us (8%)
  matrix products  30.7 us (5%)
    ppermute x12, waiting for transfers between devices, with_halo(): lax.ppermute(lax.slice_in_dim(block, 0, width, axis=dim), axis, backward)  96.3 us
    ppermute x12, starting transfers between devices, with_halo(): lax.ppermute(lax.slice_in_dim(block, 0, width, axis=dim), axis, backward)  82.8 us
    ppermute x12, waiting for transfers between devices, with_halo(): lax.ppermute(lax.slice_in_dim(block, block.shape[dim] - width, None, axis...  81.2 us
    all_gather x1, blocking collectives, per_device(): column = lax.all_gather(owned, 'gz', axis=2, tiled=True)  51.6 us
    ppermute x12, starting transfers between devices, with_halo(): lax.ppermute(lax.slice_in_dim(block, block.shape[dim] - width, None, axis...  46.6 us
    gather x1, local copies, waits for them, and re-layouts, per_device(): values = jnp.take(padded_potential.reshape(-1), flat_cells, axis=0)  45.5 us
    scatter-add x1, other arithmetic, per_device(): density = jnp.zeros((padded_shape[0] * padded_shape[1] * padded_shape[2],...  43.4 us
    unnamed x16, matrix products  20.8 us
  transfers between devices with their start and end apart: 32, of which 25 were waited for; matrix products, arithmetic and copies ran while one was open for 7% of the time, Pallas kernels for 0%

commit v1 on v0

v1 whole, which is shorter than its diff:
```python
import math

import jax
import jax.numpy as jnp
import numpy as np
from jax import lax
from jax.experimental import pallas as pl
from jax.experimental.pallas import tpu as pltpu
from jax.sharding import PartitionSpec as P

MESH = 256
GX, GY, GZ = 32, 8, 2
ATOMS, NEIGH, CHAN, SPLINE = 128, 12, 64, 64
F32, BF16, I32 = jnp.float32, jnp.bfloat16, jnp.int32
BY_MESH = pl.DeviceIdType.MESH
HIGHEST = lax.Precision.HIGHEST
VMEM = pl.BlockSpec(memory_space=pltpu.VMEM)
PLANES = tuple((da, db) for da in (-1, 0, 1) for db in (-1, 0, 1) if (da, db) != (0, 0))
ZPAD = 136
ROWS = 640


def real_basis():
    n = np.arange(MESH)[:, None]
    m = np.arange(MESH)[None, :]
    freq = np.where(m <= 128, m, m - 128)
    angle = 2.0 * np.pi * ((n * freq) % MESH) / MESH
    basis = np.where(m <= 128, np.cos(angle), np.sin(angle)) * np.sqrt(2.0 / MESH)
    basis[:, 0] = 1.0 / np.sqrt(MESH)
    basis[:, 128] /= np.sqrt(2.0)
    return basis


def tables():
    basis = real_basis()
    along_z = np.zeros((GZ, ZPAD, MESH))
    for c in range(GZ):
        along_z[c, :134] = basis[(128 * c + np.arange(134) - 3) % MESH]
    along_y = np.zeros((GY, 128, 3, MESH))
    for b in range(GY):
        for third in range(3):
            along_y[b, third * 40 : third * 40 + 38, third] = basis[
                (32 * b + np.arange(38) - 3) % MESH
            ]
    along_x = np.zeros((GX, 16, MESH))
    for a in range(GX):
        along_x[a, :14] = basis[(8 * a + np.arange(14) - 3) % MESH]
    order = np.zeros((16, 16, 3, 5, 16))
    for p in range(14):
        for k in range(16):
            order[k, p, p % 3, p // 3, k] = 1.0
    as_bf16 = lambda x: jnp.asarray(x, BF16)
    along_x = along_x.reshape(512, 256)
    order = order.reshape(256, 240)
    return dict(
        z_fwd=as_bf16(along_z.transpose(0, 2, 1)),
        z_inv=as_bf16(along_z),
        y=as_bf16(along_y.reshape(1024, 768)),
        x_fwd=as_bf16(along_x.T),
        x_inv=as_bf16(along_x),
        order=as_bf16(order),
        back=as_bf16(order.T),
    )


def dot_nn(a, b, precision=None):
    return jnp.dot(a, b, preferred_element_type=F32, precision=precision)


def dot_nt(a, b):
    return lax.dot_general(a, b, (((1,), (1,)), ((), ())), preferred_element_type=F32)


def silu(x):
    return x / (1.0 + jnp.exp(-x))


def split_rows(rows):
    block = rows >> 7
    slot = rows & 127
    ninth = (block * 43) >> 7
    oz = block - 3 * ninth - 1
    third = (ninth * 43) >> 7
    ox = third - 1
    oy = ninth - 3 * third - 1
    return ninth * 128 + slot, ox, oy, oz


def edge_sums(table, rows, counts, own_pos, same_layer, rin, rout):
    index, ox, oy, oz = split_rows(rows)
    slot = lax.broadcasted_iota(I32, (NEIGH, ATOMS), 0)
    use = (oz == 0) if same_layer else (oz != 0)
    index = jnp.where(use & (slot < counts), index, -1)
    shift = [8.0 * o.astype(F32) for o in (ox, oy, oz)]
    sums = [jnp.zeros((CHAN, 2 * ATOMS), F32) for _ in range(4)]
    rows_iota = lax.broadcasted_iota(I32, (9 * ATOMS, ATOMS), 0)
    centre = 4.0 * lax.broadcasted_iota(I32, (8, 2 * ATOMS), 0).astype(F32)
    for pair in range(NEIGH // 2):
        ks = (2 * pair, 2 * pair + 1)
        pick = jnp.concatenate(
            [jnp.where(rows_iota == index[k : k + 1], 1.0, 0.0).astype(BF16) for k in ks], axis=1
        )
        got = dot_nn(table, pick)
        delta = []
        for d in range(3):
            moved = jnp.concatenate(
                [shift[d][k : k + 1] - own_pos[d : d + 1] for k in ks], axis=1
            )
            delta.append(got[256 + d : 257 + d] + moved)
        length = jnp.sqrt(delta[0] * delta[0] + delta[1] * delta[1] + delta[2] * delta[2] + 1.0)
        unit = [d / length for d in delta]
        off = length - centre
        basis = jnp.exp(off * off * -0.125)
        hidden = silu(dot_nn(rin, basis, HIGHEST))
        radial = dot_nn(rout, hidden, HIGHEST)
        r0, r1, r2 = radial[:CHAN], radial[CHAN : 2 * CHAN], radial[2 * CHAN :]
        s = got[:CHAN]
        v = [got[CHAN * (d + 1) : CHAN * (d + 2)] for d in range(3)]
        along = unit[0] * v[0] + unit[1] * v[1] + unit[2] * v[2]
        sums[0] = sums[0] + (r0 * s + r2 * along)
        turned = r1 * s
        for d in range(3):
            sums[d + 1] = sums[d + 1] + (turned * unit[d] + r2 * v[d])
    return [x[:, :ATOMS] + x[:, ATOMS:] for x in sums]


def atom_kernel(
    feat, pos, nbr, cnt, rin, rout, mixes, head, updated, charge,
    mine, table, pos_pad, ask, ask_in, pos_in, part, part_in, send, recv, far_send, far_recv,
):
    a, b, c = lax.axis_index("gx"), lax.axis_index("gy"), lax.axis_index("gz")
    other = {"gz": 1 - c}
    barrier = pltpu.get_barrier_semaphore()

    def plane(da, db):
        return {"gx": lax.rem(a + da + GX, GX), "gy": lax.rem(b + db + GY, GY)}

    for da, db in PLANES:
        pl.semaphore_signal(barrier, inc=1, device_id=plane(da, db), device_id_type=BY_MESH)
    pl.semaphore_signal(barrier, inc=1, device_id=other, device_id_type=BY_MESH)

    own = feat[...].astype(F32).T
    mine[:256, :] = own.astype(BF16)
    pos_pad[...] = jnp.zeros_like(pos_pad)
    pos_pad[:3, :] = pos[...].astype(F32)
    mine[256:, :] = pos_pad[...].astype(BF16)
    ask[...] = jnp.zeros_like(ask)
    ask[:NEIGH, :] = nbr[...]
    ask[NEIGH : NEIGH + 1, :] = cnt[...]
    pl.semaphore_wait(barrier, len(PLANES) + 1)

    def far(source, target, i):
        return pltpu.make_async_remote_copy(
            source, target, far_send.at[i], far_recv.at[i], device_id=other, device_id_type=BY_MESH
        )

    asks = [far(ask, ask_in, 0), far(mine.at[256:], pos_in, 1)]
    for copy in asks:
        copy.start()
    copies = []
    for i, (da, db) in enumerate(PLANES):
        place = (1 - da) * 3 + (1 - db)
        copies.append(
            pltpu.make_async_remote_copy(
                mine,
                table.at[:, place * ATOMS : (place + 1) * ATOMS],
                send.at[i],
                recv.at[i],
                device_id=plane(da, db),
                device_id_type=BY_MESH,
            )
        )
    for copy in copies:
        copy.start()
    table[:, 4 * ATOMS : 5 * ATOMS] = mine[...]
    for copy in asks + copies:
        copy.wait()
    known = table[...]
    their = ask_in[...]
    sums = edge_sums(
        known, their[:NEIGH], their[NEIGH : NEIGH + 1], pos_in[...].astype(F32), False,
        rin[...], rout[...],
    )
    for i in range(4):
        part[i * CHAN : (i + 1) * CHAN, :] = sums[i].astype(BF16)
    partial = far(part, part_in, 2)
    partial.start()
    sums = edge_sums(
        known, nbr[...], cnt[...], pos_pad[...], True, rin[...], rout[...]
    )
    partial.wait()
    agg = [
        ((sums[i] + part_in[i * CHAN : (i + 1) * CHAN, :].astype(F32)) / NEIGH).astype(BF16)
        for i in range(4)
    ]
    mix = mixes[...]
    mixed = dot_nn(mix[: 2 * CHAN], agg[0])
    gate = 1.0 / (1.0 + jnp.exp(-mixed[CHAN:]))
    scalars = own[:CHAN] + silu(mixed[:CHAN])
    vectors = [
        own[CHAN * (d + 1) : CHAN * (d + 2)] + dot_nn(mix[2 * CHAN :], agg[d + 1]) * gate
        for d in range(3)
    ]
    result = jnp.concatenate([scalars] + vectors, axis=0).astype(BF16).astype(F32)
    updated[...] = result.T.astype(BF16)
    charge[...] = jnp.sum(head[...] * result[:CHAN], axis=0, keepdims=True)


def cell_rows(cells):
    p, q = cells[0], cells[1]
    return p * 40 + 8 * ((p * 43) >> 7) + q


def spread_kernel(cells, weight, charge, z_fwd, out, density):
    c = lax.axis_index("gz")
    density[...] = jnp.zeros_like(density)
    group = 8
    rows_iota = lax.broadcasted_iota(I32, (ROWS, ATOMS), 0)
    z_iota = lax.broadcasted_iota(I32, (ZPAD, ATOMS), 0)

    @pl.loop(0, SPLINE // group)
    def _(step):
        span = pl.ds(pl.multiple_of(step * group, group), group)
        place = cell_rows([cells[0, span, :], cells[1, span, :]])
        depth = cells[2, span, :]
        value = weight[span, :] * charge[...]
        pick = jnp.concatenate(
            [
                jnp.where(rows_iota == place[k : k + 1], 1.0, 0.0).astype(BF16)
                for k in range(group)
            ],
            axis=1,
        )
        spot = jnp.concatenate(
            [
                jnp.where(z_iota == depth[k : k + 1], value[k : k + 1], 0.0).astype(BF16)
                for k in range(group)
            ],
            axis=1,
        )
        density[...] += dot_nt(pick, spot)

    matrix = z_fwd[c]
    for g in range(5):
        block = density[g * 128 : (g + 1) * 128, :].astype(BF16)
        out[g, :, :] = dot_nt(matrix, block).astype(BF16)


def mesh_kernel(
    modes, y_mat, x_fwd, x_inv, order, back, z_inv, out,
    in1, out2, in2, out3, in3, out4, in4, send1, recv1, send2, recv2, send3, recv3, send4, recv4,
):
    a, b, c = lax.axis_index("gx"), lax.axis_index("gy"), lax.axis_index("gz")
    me = c * GY + b
    near, wide = GY * GZ, GX
    barrier = pltpu.get_barrier_semaphore()

    def near_id(i):
        return {"gy": lax.rem(i, GY), "gz": i // GY}

    @pl.loop(1, near)
    def _(d):
        pl.semaphore_signal(
            barrier, inc=1, device_id=near_id(lax.rem(me + d, near)), device_id_type=BY_MESH
        )

    @pl.loop(1, wide)
    def _(d):
        pl.semaphore_signal(
            barrier, inc=1, device_id={"gx": lax.rem(a + d, wide)}, device_id_type=BY_MESH
        )

    def tile(i, size):
        return pl.ds(pl.multiple_of(i * size, size), size)

    def exchange(count, here, source, target, send, recv, device):
        def copy(to, frm, i):
            return pltpu.make_async_remote_copy(
                source(to), target(frm), send.at[i], recv.at[frm],
                device_id=device(to), device_id_type=BY_MESH,
            )

        @pl.loop(1, count)
        def _(d):
            copy(lax.rem(here + d, count), here, d).start()

        target(here)[...] = source(here)[...]

        @pl.loop(1, count)
        def _(d):
            copy(lax.rem(here + d, count), lax.rem(here + d, count), d).wait_recv()

        @pl.loop(1, count)
        def _(d):
            copy(lax.rem(here + d, count), here, d).wait_send()

    def wide_id(i):
        return {"gx": i}

    signed = lambda i: jnp.where(i <= 128, i, i - 128).astype(F32)
    kz = me * 16 + a // 2
    ky = lax.rem(a, 2) * 128 + lax.broadcasted_iota(I32, (MESH, 128), 1)
    kx = lax.broadcasted_iota(I32, (MESH, 128), 0)
    fz = jnp.where(kz <= 128, kz, kz - 128).astype(F32)
    step_size = 2.0 * math.pi / MESH
    screen = 4.0 * math.pi / MESH
    fx, fy = signed(kx), signed(ky)
    ksquare = step_size * step_size * (fx * fx + fy * fy + fz * fz)
    green = jnp.exp(-0.5 * ksquare) / (ksquare + screen * screen)
    green = jnp.where((kx + ky + kz) == 0, 0.0, green)

    pl.semaphore_wait(barrier, near - 1 + wide - 1)

    exchange(
        near, me,
        lambda to: modes.at[:, tile(to, 16), :],
        lambda frm: in1.at[frm // GY, :, :, tile(lax.rem(frm, GY), 128)],
        send1, recv1, near_id,
    )
    matrix = y_mat[...]
    mixed = dot_nn(in1[0].reshape(80, 1024), matrix) + dot_nn(in1[1].reshape(80, 1024), matrix)
    stacked = jnp.concatenate(
        [mixed[:, i * MESH : (i + 1) * MESH].astype(BF16) for i in range(3)], axis=0
    )
    out2[...] = dot_nn(order[...], stacked).astype(BF16)

    def grid_tile(ref):
        return lambda i: ref.at[tile(i // 2, 16), tile(lax.rem(i, 2), 128)]

    def row_tile(ref):
        return lambda i: ref.at[tile(i, 16), :]

    exchange(wide, a, grid_tile(out2), row_tile(in2), send2, recv2, wide_id)
    spectrum = dot_nn(x_fwd[...], in2[...]) * green
    out3[...] = dot_nn(x_inv[...], spectrum.astype(BF16)).astype(BF16)
    exchange(wide, a, row_tile(out3), grid_tile(in3), send3, recv3, wide_id)
    stacked = dot_nn(back[...], in3[...]).astype(BF16)
    joined = jnp.concatenate([stacked[80 * i : 80 * (i + 1)] for i in range(3)], axis=1)
    out4[...] = dot_nt(joined, matrix).astype(BF16).reshape(5, 16, 1024)
    exchange(
        near, me,
        lambda to: out4.at[:, :, tile(lax.rem(to, GY), 128)],
        lambda frm: in4.at[:, tile(frm, 16), :],
        send4, recv4, near_id,
    )
    matrix = z_inv[c]
    for g in range(5):
        out[:, g * 128 : (g + 1) * 128] = dot_nn(matrix, in4[g]).astype(BF16)


def force_kernel(cells, slope, charge, potential, out, values):
    group = 8
    rows_iota = lax.broadcasted_iota(I32, (ROWS, ATOMS), 0)
    z_iota = lax.broadcasted_iota(I32, (ZPAD, ATOMS), 0)
    field = potential[...]

    @pl.loop(0, SPLINE // group)
    def _(step):
        span = pl.ds(pl.multiple_of(step * group, group), group)
        place = cell_rows([cells[0, span, :], cells[1, span, :]])
        depth = cells[2, span, :]
        pick = jnp.concatenate(
            [
                jnp.where(rows_iota == place[k : k + 1], 1.0, 0.0).astype(BF16)
                for k in range(group)
            ],
            axis=1,
        )
        lines = dot_nn(field, pick)
        values[span, :] = jnp.concatenate(
            [
                jnp.sum(
                    jnp.where(
                        z_iota == depth[k : k + 1], lines[:, k * ATOMS : (k + 1) * ATOMS], 0.0
                    ),
                    axis=0,
                    keepdims=True,
                )
                for k in range(group)
            ],
            axis=0,
        )

    found = values[...]
    for d in range(3):
        out[d : d + 1, :] = -charge[...] * jnp.sum(slope[d] * found, axis=0, keepdims=True)


LIMIT = 40 * 1024 * 1024
DMA = pltpu.SemaphoreType.DMA


def per_device(
    features, positions, neighbours, counts, cell_index, spline_weight, spline_slope,
    radial_in, radial_out, mix_scalar, mix_vector, mix_gate, charge_head,
):
    tab = tables()
    cells, weight, slope = cell_index[0, 0, 0], spline_weight[0, 0, 0], spline_slope[0, 0, 0]
    mixes = jnp.concatenate([mix_scalar.T, mix_gate.T, mix_vector.T], axis=0)
    updated, charge = pl.pallas_call(
        atom_kernel,
        out_shape=(
            jax.ShapeDtypeStruct((ATOMS, 4 * CHAN), BF16),
            jax.ShapeDtypeStruct((1, ATOMS), F32),
        ),
        in_specs=[VMEM] * 8,
        out_specs=(VMEM, VMEM),
        scratch_shapes=[
            pltpu.VMEM((272, ATOMS), BF16),
            pltpu.VMEM((272, 9 * ATOMS), BF16),
            pltpu.VMEM((16, ATOMS), F32),
            pltpu.VMEM((16, ATOMS), I32),
            pltpu.VMEM((16, ATOMS), I32),
            pltpu.VMEM((16, ATOMS), BF16),
            pltpu.VMEM((256, ATOMS), BF16),
            pltpu.VMEM((256, ATOMS), BF16),
            DMA((8,)),
            DMA((8,)),
            DMA((3,)),
            DMA((3,)),
        ],
        compiler_params=pltpu.CompilerParams(
            collective_id=0, has_side_effects=True, vmem_limit_bytes=LIMIT
        ),
        name="atoms",
    )(
        features[0, 0, 0], positions[0, 0, 0], neighbours[0, 0, 0], counts[0, 0],
        radial_in.T, radial_out.T, mixes, charge_head[:, None],
    )
    modes = pl.pallas_call(
        spread_kernel,
        out_shape=jax.ShapeDtypeStruct((5, MESH, 128), BF16),
        in_specs=[VMEM] * 4,
        out_specs=VMEM,
        scratch_shapes=[pltpu.VMEM((ROWS, ZPAD), F32)],
        compiler_params=pltpu.CompilerParams(vmem_limit_bytes=LIMIT),
        name="spread",
    )(cells, weight, charge, tab["z_fwd"])
    near, wide = GY * GZ, GX
    potential = pl.pallas_call(
        mesh_kernel,
        out_shape=jax.ShapeDtypeStruct((ZPAD, ROWS), BF16),
        in_specs=[VMEM] * 7,
        out_specs=VMEM,
        scratch_shapes=[
            pltpu.VMEM((2, 5, 16, 1024), BF16),
            pltpu.VMEM((256, 256), BF16),
            pltpu.VMEM((512, 128), BF16),
            pltpu.VMEM((512, 128), BF16),
            pltpu.VMEM((256, 256), BF16),
            pltpu.VMEM((5, 16, 1024), BF16),
            pltpu.VMEM((5, 256, 128), BF16),
            DMA((near,)), DMA((near,)), DMA((wide,)), DMA((wide,)),
            DMA((wide,)), DMA((wide,)), DMA((near,)), DMA((near,)),
        ],
        compiler_params=pltpu.CompilerParams(
            collective_id=1, has_side_effects=True, vmem_limit_bytes=LIMIT
        ),
        name="mesh",
    )(modes, tab["y"], tab["x_fwd"], tab["x_inv"], tab["order"], tab["back"], tab["z_inv"])
    forces = pl.pallas_call(
        force_kernel,
        out_shape=jax.ShapeDtypeStruct((3, ATOMS), F32),
        in_specs=[VMEM] * 4,
        out_specs=VMEM,
        scratch_shapes=[pltpu.VMEM((SPLINE, ATOMS), F32)],
        compiler_params=pltpu.CompilerParams(vmem_limit_bytes=LIMIT),
        name="forces",
    )(cells, slope, charge, potential)
    return (updated[None, None, None], forces[None, None, None])


def solution(mesh):
    placed = (
        P("gx", "gy", "gz", None, None),
        P("gx", "gy", "gz", None, None),
        P("gx", "gy", "gz", None, None),
        P("gx", "gy", "gz", None),
        P("gx", "gy", "gz", None, None, None),
        P("gx", "gy", "gz", None, None),
        P("gx", "gy", "gz", None, None, None),
        P(), P(), P(), P(), P(), P(),
    )
    return jax.shard_map(
        per_device,
        mesh=mesh,
        in_specs=placed,
        out_specs=(P("gx", "gy", "gz", None, None), P("gx", "gy", "gz", None, None)),
        check_vma=False,
    )
```

time: 643 us -> 133 us (0.21); the launches traced: 635 us -> 132 us
  waiting for transfers between devices: 223 us -> 0 us
  starting transfers between devices: 185 us -> 0 us
  Pallas kernels: 0 us -> 116 us
  local copies, waits for them, and re-layouts: 79.3 us -> 14.8 us
  other arithmetic: 62.4 us -> 0.02 us
  blocking collectives: 51.6 us -> 0 us
  matrix products: 30.7 us -> 0 us
    ppermute x24 -> x0, waiting for transfers between devices: 178 us -> none  [the longest x12 96.3 us: with_halo(): lax.ppermute(lax.slice_in_dim(block, 0, width, axis=dim), axis, backward)]
    ppermute x24 -> x0, starting transfers between devices: 129 us -> none  [the longest x12 82.8 us: with_halo(): lax.ppermute(lax.slice_in_dim(block, 0, width, axis=dim), axis, backward)]
    pallas_call x0 -> x4, Pallas kernels: none -> 116 us  [the longest x1 66.1 us: per_device(): pl.pallas_call(mesh_kernel, out_shape=jax.ShapeDtypeStruct((ZPAD, ROWS),...]
    all_to_all x8 -> x0, starting transfers between devices: 55.8 us -> none  [the longest x1 16.3 us: per_device(): lax.all_to_all(real_part.astype(jnp.bfloat16), 'gx', split_axis=1, concat...]
    gather x4 -> x0, local copies, waits for them, and re-layouts: 53.3 us -> none  [the longest x1 45.5 us: per_device(): values = jnp.take(padded_potential.reshape(-1), flat_cells, axis=0)]
    all_gather x1 -> x0, blocking collectives: 51.6 us -> none  [per_device(): column = lax.all_gather(owned, 'gz', axis=2, tiled=True)]
    all_to_all x8 -> x0, waiting for transfers between devices: 45.4 us -> none  [the longest x1 8.99 us: per_device(): lax.all_to_all(real_part.astype(jnp.bfloat16), 'gx', split_axis=0, concat...]
    scatter-add x1 -> x0, other arithmetic: 43.4 us -> none  [per_device(): density = jnp.zeros((padded_shape[0] * padded_shape[1] * padded_shape[2],...]
  transfers between devices with their start and end apart: 32 -> 0, of which waited for: 25 -> 0; matrix products, arithmetic and copies ran while one was open for 7% -> 0% of each run, Pallas kernels for 0% -> 0%
where the time goes in v1:
time: 133 us; the launch traced here: 132 us
  Pallas kernels  116 us (87%)
  local copies, waits for them, and re-layouts  14.8 us (11%)
    pallas_call x1, Pallas kernels, per_device(): pl.pallas_call(mesh_kernel, out_shape=jax.ShapeDtypeStruct((ZPAD, ROWS),...  66.1 us
    pallas_call x1, Pallas kernels, per_device(): pl.pallas_call(atom_kernel, out_shape=(jax.ShapeDtypeStruct((ATOMS, 4 * C...  42.2 us
    unnamed x34, local copies, waits for them, and re-layouts  14.1 us
    pallas_call x1, Pallas kernels, per_device(): pl.pallas_call(spread_kernel, out_shape=jax.ShapeDtypeStruct((5, MESH, 12...  4.53 us
    pallas_call x1, Pallas kernels, per_device(): pl.pallas_call(force_kernel, out_shape=jax.ShapeDtypeStruct((3, ATOMS), F...  3.51 us

profile of v1, /device:TPU:1, one launch (start us, length us, event | category | flops | bytes accessed | tf_op | source)
XLA Modules:
  0.0 132.0 jit_solution(3769434476873838908)
XLA Ops:
  0.6 0.0 copy-start.2
  0.6 0.0 copy-start.3
  0.7 0.0 copy-start.5
  0.7 0.8 copy.31
  1.4 0.8 copy.24
  2.2 0.8 copy.26
  3.0 0.8 copy.25
  3.9 0.8 copy.22
  4.7 0.7 copy.27.head
  5.4 0.9 copy.23
  6.3 0.0 copy-start.9
  6.3 0.8 copy-done.9
  7.2 0.7 copy-done.11
  7.9 0.7 copy-done.12
  8.5 42.2 %atoms.1 = (bf16[128,256]{1,0:T(8,128)(2,1)S(1)}, f32[1,128]{1,0:T(1,128)S(1)}) custom-call(bf16[128,256]{1,0:T(8,128)(2,1)S(1)} %bitcast.23, bf16[3,128]{1,0:T(4,128)(2,1)S(1)} %bitcast.27, s32[12,128]{1,0:T(8,128)S(1)} %bitcast.25, s32[1,128]{1,0:T(1,128)S(1)} %bitcast.28, f32[64,8]{1,0:T(8,128)S(1)} %bitcast.20, f32[192,64]{1,0:T(8,128)S(1)} %bitcast.19, ...), custom_call_target="tpu_custom_call" | custom-call | tf_op jit(solution)/shard_map/atoms/pallas_call | solution.py:400
  50.7 0.0 copy-start.1
  50.8 0.9 copy-done.1
  51.6 0.9 copy-done.4
  52.6 0.8 copy-done.10
  53.4 4.5 %spread.1.modes = bf16[5,256,128]{2,1,0:T(8,128)(2,1)S(1)} custom-call(s32[3,64,128]{2,1,0:T(8,128)S(1)} %bitcast.17, f32[64,128]{1,0:T(8,128)S(1)} %bitcast.24, f32[1,128]{1,0:T(1,128)S(1)} %get-tuple-element.5.charge, bf16[2,256,136]{2,1,0:T(8,128)(2,1)S(1)} %copy-done.4), custom_call_target="tpu_custom_call" | custom-call | tf_op jit(solution)/shard_map/spread/pallas_call | solution.py:430
  57.9 0.0 copy-done.2
  57.9 0.0 copy-done.3
  57.9 0.0 copy-done.5
  57.9 0.0 copy-start
  57.9 1.4 %copy-done = bf16[1024,768]{1,0:T(8,128)(2,1)S(1)} copy-done((bf16[1024,768]{1,0:T(8,128)(2,1)S(1)}, bf16[1024,768]{1,0:T(8,128)(2,1)}, u32[]{:S(2)}) %copy-start) | copy-done | bytes 1572888
  59.3 0.9 copy-done.6
  60.2 0.9 copy-done.7
  61.1 66.1 %mesh.1.potential = bf16[136,640]{1,0:T(8,128)(2,1)S(1)} custom-call(bf16[5,256,128]{2,1,0:T(8,128)(2,1)S(1)} %spread.1.modes, bf16[1024,768]{1,0:T(8,128)(2,1)S(1)} %copy-done, bf16[256,512]{1,0:T(8,128)(2,1)S(1)} %copy-done.3, bf16[512,256]{1,0:T(8,128)(2,1)S(1)} %copy-done.2, bf16[256,240]{1,0:T(8,128)(2,1)S(1)} %copy-done.6, ...), custom_call_target="tpu_custom_call" | custom-call | tf_op jit(solution)/shard_map/mesh/pallas_call | solution.py:440
  127.2 0.0 copy-done.8
  127.3 3.5 %forces.1 = f32[3,128]{1,0:T(4,128)S(1)} custom-call(s32[3,64,128]{2,1,0:T(8,128)S(1)} %bitcast.18, f32[3,64,128]{2,1,0:T(8,128)S(1)} %bitcast.21, f32[1,128]{1,0:T(1,128)S(1)} %get-tuple-element.5.charge, bf16[136,640]{1,0:T(8,128)(2,1)S(1)} %mesh.1.potential), custom_call_target="tpu_custom_call" | custom-call | tf_op jit(solution)/shard_map/forces/pallas_call | solution.py:461
  130.8 0.6 copy.28
  131.3 0.6 copy.33
  (8 shorter events, 0.0 us)
Async XLA Ops:
  0.6 57.3 %copy-start.2 = (bf16[512,256]{1,0:T(8,128)(2,1)S(1)}, bf16[512,256]{1,0:T(8,128)(2,1)}, u32[]{:S(2)}) copy-start(bf16[512,256]{1,0:T(8,128)(2,1)} %constant.18.clone.x_inv) | copy-start | bytes 786436
  0.6 57.3 %copy-start.3 = (bf16[256,512]{1,0:T(8,128)(2,1)S(1)}, bf16[256,512]{1,0:T(8,128)(2,1)}, u32[]{:S(2)}) copy-start(bf16[256,512]{1,0:T(8,128)(2,1)} %constant.17.clone.x_fwd) | copy-start | bytes 786436
  0.7 57.3 %copy-start.5 = (bf16[2,136,256]{2,1,0:T(8,128)(2,1)S(1)}, bf16[2,136,256]{2,1,0:T(8,128)(2,1)}, u32[]{:S(2)}) copy-start(bf16[2,136,256]{2,1,0:T(8,128)(2,1)} %constant.15.clone.z_inv) | copy-start | bytes 417796
  6.3 0.8 copy-start.9
  7.2 0.7 copy-start.11
  7.9 0.7 copy-start.12
  50.7 0.9 copy-start.1
  51.6 0.9 copy-start.4
  52.6 0.8 copy-start.10
  57.9 1.4 %copy-start = (bf16[1024,768]{1,0:T(8,128)(2,1)S(1)}, bf16[1024,768]{1,0:T(8,128)(2,1)}, u32[]{:S(2)}) copy-start(bf16[1024,768]{1,0:T(8,128)(2,1)} %constant.16.clone.y_mat) | copy-start | bytes 4718596
  59.3 0.9 copy-start.6
  60.2 0.9 copy-start.7
  61.1 66.1 %copy-start.8 = (f32[1,1,1,3,64,128]{5,4,3,2,1,0:T(8,128)S(1)}, f32[1,1,1,3,64,128]{5,4,3,2,1,0:T(8,128)}, u32[]{:S(2)}) copy-start(f32[1,1,1,3,64,128]{5,4,3,2,1,0:T(8,128)} %param.26) | copy-start | bytes 294916

commit v2 on v1

v2 whole, which is shorter than its diff:
```python
import math

import jax
import jax.numpy as jnp
import numpy as np
from jax import lax
from jax.experimental import pallas as pl
from jax.experimental.pallas import tpu as pltpu
from jax.sharding import PartitionSpec as P

MESH = 256
GX, GY, GZ = 32, 8, 2
ATOMS, NEIGH, CHAN, SPLINE = 128, 12, 64, 64
F32, BF16, I32 = jnp.float32, jnp.bfloat16, jnp.int32
BY_MESH = pl.DeviceIdType.MESH
HIGHEST = lax.Precision.HIGHEST
VMEM = pl.BlockSpec(memory_space=pltpu.VMEM)
ANY = pl.BlockSpec(memory_space=pl.ANY)
PLANES = tuple((da, db) for da in (-1, 0, 1) for db in (-1, 0, 1) if (da, db) != (0, 0))
ZPAD = 136
ROWS = 640
GROUP = 8
CHUNKS = SPLINE // GROUP
WIDTH = GROUP * ATOMS


def real_basis():
    n = np.arange(MESH)[:, None]
    m = np.arange(MESH)[None, :]
    freq = np.where(m <= 128, m, m - 128)
    angle = 2.0 * np.pi * ((n * freq) % MESH) / MESH
    basis = np.where(m <= 128, np.cos(angle), np.sin(angle)) * np.sqrt(2.0 / MESH)
    basis[:, 0] = 1.0 / np.sqrt(MESH)
    basis[:, 128] /= np.sqrt(2.0)
    return basis


def tables():
    basis = real_basis()
    along_z = np.zeros((GZ, ZPAD, MESH))
    for c in range(GZ):
        along_z[c, :134] = basis[(128 * c + np.arange(134) - 3) % MESH]
    along_y = np.zeros((GY, 128, 3, MESH))
    for b in range(GY):
        for third in range(3):
            along_y[b, third * 40 : third * 40 + 38, third] = basis[
                (32 * b + np.arange(38) - 3) % MESH
            ]
    along_x = np.zeros((GX, 16, MESH))
    for a in range(GX):
        along_x[a, :14] = basis[(8 * a + np.arange(14) - 3) % MESH]
    order = np.zeros((16, 16, 3, 5, 16))
    for p in range(14):
        for k in range(16):
            order[k, p, p % 3, p // 3, k] = 1.0
    as_bf16 = lambda x: jnp.asarray(x, BF16)
    along_x = along_x.reshape(512, 256)
    order = order.reshape(256, 240)
    halves = along_z.reshape(GZ, ZPAD, 2, 128)
    return [
        as_bf16(halves.transpose(2, 0, 3, 1)),
        as_bf16(halves.transpose(2, 0, 1, 3)),
        as_bf16(along_y.reshape(1024, 768)),
        as_bf16(along_x.T),
        as_bf16(along_x),
        as_bf16(order),
        as_bf16(order.T),
    ]


def dot_nn(a, b, precision=None):
    return jnp.dot(a, b, preferred_element_type=F32, precision=precision)


def dot_nt(a, b):
    return lax.dot_general(a, b, (((1,), (1,)), ((), ())), preferred_element_type=F32)


def dot_tn(a, b):
    return lax.dot_general(a, b, (((0,), (0,)), ((), ())), preferred_element_type=F32)


def halves_of(x):
    high = x.astype(BF16).astype(F32)
    return high, x - high


def silu(x):
    return x / (1.0 + jnp.exp(-x))


def split_rows(rows):
    block = rows >> 7
    slot = rows & 127
    ninth = (block * 43) >> 7
    oz = block - 3 * ninth - 1
    third = (ninth * 43) >> 7
    ox = third - 1
    oy = ninth - 3 * third - 1
    return ninth * 128 + slot, ox, oy, oz


def fill_pick(pick, rows, counts, same_layer):
    index, ox, oy, oz = split_rows(rows)
    slot = lax.broadcasted_iota(I32, (NEIGH, ATOMS), 0)
    use = (oz == 0) if same_layer else (oz != 0)
    index = jnp.where(use & (slot < counts), index, -1)
    rows_iota = lax.broadcasted_iota(I32, (9 * ATOMS, ATOMS), 0)
    for k in range(NEIGH):
        pick[:, k * ATOMS : (k + 1) * ATOMS] = jnp.where(
            rows_iota == index[k : k + 1], 1.0, 0.0
        ).astype(BF16)
    return [8.0 * o.astype(F32) for o in (ox, oy, oz)]


def fill_radial(radial, units, pick, places, shift, own_pos, rin, rout):
    centre = 4.0 * lax.broadcasted_iota(I32, (8, 2 * ATOMS), 0).astype(F32)
    known = places[...]
    for pair in range(NEIGH // 2):
        ks = (2 * pair, 2 * pair + 1)
        span = slice(2 * pair * ATOMS, (2 * pair + 2) * ATOMS)
        got = dot_nn(known, pick[:, span])
        delta = []
        for d in range(3):
            moved = jnp.concatenate(
                [shift[d][k : k + 1] - own_pos[d : d + 1] for k in ks], axis=1
            )
            delta.append(got[d : d + 1] + moved)
        length = jnp.sqrt(delta[0] * delta[0] + delta[1] * delta[1] + delta[2] * delta[2] + 1.0)
        inverse = 1.0 / length
        for d in range(3):
            units[d : d + 1, span] = delta[d] * inverse
        off = length - centre
        high, low = halves_of(jnp.exp(off * off * -0.125))
        basis = jnp.concatenate([high, low, high, jnp.zeros_like(high)], axis=0).astype(BF16)
        high, low = halves_of(silu(dot_tn(rin, basis)))
        hidden = jnp.concatenate([high, low, high], axis=0).astype(BF16)
        radial[:, span] = dot_tn(rout, hidden)


def edge_sums(table, pick, radial, units):
    sums = [jnp.zeros((CHAN, 2 * ATOMS), F32) for _ in range(4)]
    known = table[...]
    for pair in range(NEIGH // 2):
        span = slice(2 * pair * ATOMS, (2 * pair + 2) * ATOMS)
        got = dot_nn(known, pick[:, span])
        r0 = radial[:CHAN, span]
        r1 = radial[CHAN : 2 * CHAN, span]
        r2 = radial[2 * CHAN :, span]
        unit = [units[d : d + 1, span] for d in range(3)]
        s = got[:CHAN]
        v = [got[CHAN * (d + 1) : CHAN * (d + 2)] for d in range(3)]
        along = unit[0] * v[0] + unit[1] * v[1] + unit[2] * v[2]
        sums[0] = sums[0] + (r0 * s + r2 * along)
        turned = r1 * s
        for d in range(3):
            sums[d + 1] = sums[d + 1] + (turned * unit[d] + r2 * v[d])
    return [x[:, :ATOMS] + x[:, ATOMS:] for x in sums]


def fill_cells(spots, cells):
    rows_iota = lax.broadcasted_iota(I32, (ROWS, ATOMS), 0)

    @pl.loop(0, CHUNKS)
    def _(step):
        span = pl.ds(pl.multiple_of(step * GROUP, GROUP), GROUP)
        p, q = cells[0, span, :], cells[1, span, :]
        place = p * 40 + 8 * ((p * 43) >> 7) + q
        for k in range(GROUP):
            spots[step, :, k * ATOMS : (k + 1) * ATOMS] = jnp.where(
                rows_iota == place[k : k + 1], 1.0, 0.0
            ).astype(BF16)


def spread(density, spots, cells, value):
    z_iota = lax.broadcasted_iota(I32, (ZPAD, ATOMS), 0)
    density[...] = jnp.zeros_like(density)

    @pl.loop(0, CHUNKS)
    def _(step):
        span = pl.ds(pl.multiple_of(step * GROUP, GROUP), GROUP)
        depth = cells[2, span, :]
        amount = value[span, :]
        lines = jnp.concatenate(
            [
                jnp.where(z_iota == depth[k : k + 1], amount[k : k + 1], 0.0).astype(BF16)
                for k in range(GROUP)
            ],
            axis=1,
        )
        density[...] += dot_nt(spots[step], lines)


def collect(values, spots, cells, field):
    z_iota = lax.broadcasted_iota(I32, (ZPAD, ATOMS), 0)

    @pl.loop(0, CHUNKS)
    def _(step):
        span = pl.ds(pl.multiple_of(step * GROUP, GROUP), GROUP)
        depth = cells[2, span, :]
        lines = dot_nn(field[...], spots[step])
        values[span, :] = jnp.concatenate(
            [
                jnp.sum(
                    jnp.where(
                        z_iota == depth[k : k + 1], lines[:, k * ATOMS : (k + 1) * ATOMS], 0.0
                    ),
                    axis=0,
                    keepdims=True,
                )
                for k in range(GROUP)
            ],
            axis=0,
        )


def tile(i, size):
    return pl.ds(pl.multiple_of(i * size, size), size)


def signed(i):
    return jnp.where(i <= 128, i, i - 128).astype(F32)


class Exchange:
    def __init__(self, count, here, source, target, send, recv, device):
        self.count, self.here, self.source, self.target = count, here, source, target
        self.send, self.recv, self.device = send, recv, device

    def copy(self, to, frm, i):
        return pltpu.make_async_remote_copy(
            self.source(to), self.target(frm), self.send.at[i], self.recv.at[frm],
            device_id=self.device(to), device_id_type=BY_MESH,
        )

    def run(self):
        count, here = self.count, self.here

        @pl.loop(1, count)
        def _(d):
            self.copy(lax.rem(here + d, count), here, d).start()

        self.target(here)[...] = self.source(here)[...]

        @pl.loop(1, count)
        def _(d):
            frm = lax.rem(here + d, count)
            self.copy(frm, frm, d).wait_recv()

    def finish(self):
        @pl.loop(1, self.count)
        def _(d):
            self.copy(lax.rem(self.here + d, self.count), self.here, d).wait_send()


def whole_kernel(
    feat, pos, nbr, cnt, cells_in, weight_in, slope_in, rin_in, rout_in, mix_s_in, mix_v_in,
    mix_g_in, head, *rest,
):
    consts_in, rest = rest[:7], rest[7:]
    (updated, forces), rest = rest[:2], rest[2:]
    loads, rest = rest[:16], rest[16:]
    (
        own_feat, rows_in, cells, weight, slope, rin_v, rout_v, mix_s, mix_v, mix_g
    ) = loads[:9] + loads[9:10]
    z_fwd, z_inv, y_mat, x_fwd, x_inv, order = loads[10:16]
    (
        back, load_sem, mine, table, places, pos_pad, ask, ask_in, pos_in, own_in, part, part_in,
        same, same_in, points, points_in, cells_par, pick_own, pick_par, radial_own, radial_par,
        units_own, units_par, spots_own, spots_par, value, density_own, density_par, modes, in1,
        out2, in2, out3, in3, out4, in4, field, values, force, force_in,
        pos_send, pos_recv, send, recv, far_send, far_recv,
        send1, recv1, send2, recv2, send3, recv3, send4, recv4,
    ) = rest
    a, b, c = lax.axis_index("gx"), lax.axis_index("gy"), lax.axis_index("gz")
    other = {"gz": 1 - c}
    barrier = pltpu.get_barrier_semaphore()

    inputs = [feat, nbr, cells_in, weight_in, slope_in, rin_in, rout_in, mix_s_in, mix_v_in, mix_g_in]
    fetch = [
        pltpu.make_async_copy(source, target, load_sem.at[i])
        for i, (source, target) in enumerate(
            zip(inputs + list(consts_in), list(loads) + [back])
        )
    ]
    for copy in fetch:
        copy.start()

    def plane(da, db):
        return {"gx": lax.rem(a + da + GX, GX), "gy": lax.rem(b + db + GY, GY)}

    def gy_id(i):
        return {"gy": i}

    def gx_id(i):
        return {"gx": i}

    def greet(device):
        pl.semaphore_signal(barrier, inc=1, device_id=device, device_id_type=BY_MESH)

    greet(other)
    for da, db in PLANES:
        if da and db:
            greet(plane(da, db))

    @pl.loop(1, GX)
    def _(d):
        greet(gx_id(lax.rem(a + d, GX)))

    @pl.loop(1, GY)
    def _(d):
        greet(gy_id(lax.rem(b + d, GY)))

    fetch[0].wait()
    own = own_feat[...].astype(F32).T
    mine[...] = own.astype(BF16)
    pos_pad[...] = jnp.zeros_like(pos_pad)
    pos_pad[:3, :] = pos[...].astype(F32)
    own_pos16 = pos_pad[...].astype(BF16)
    places[:, 4 * ATOMS : 5 * ATOMS] = own_pos16
    table[:, 4 * ATOMS : 5 * ATOMS] = mine[...]
    fetch[1].wait()
    ask[...] = jnp.zeros_like(ask)
    for k in range(NEIGH):
        ask[k : k + 1, :] = rows_in[k]
    ask[NEIGH : NEIGH + 1, :] = cnt[...]
    for copy in fetch[2:5]:
        copy.wait()
    for d in range(3):
        points[d] = cells[d].astype(F32).astype(BF16)
        points[4 + d] = slope[d].astype(BF16)
    points[3] = weight[...].astype(BF16)
    for copy in fetch[5:]:
        copy.wait()
    high, low = halves_of(rin_v[...])
    rin = jnp.concatenate([high, high, low, jnp.zeros_like(high)], axis=0).astype(BF16)
    high, low = halves_of(rout_v[...])
    rout = jnp.concatenate([high, high, low], axis=0).astype(BF16)

    pl.semaphore_wait(barrier, 1 + 4 + GX - 1 + GY - 1)

    def far(source, target, i):
        return pltpu.make_async_remote_copy(
            source, target, far_send.at[i], far_recv.at[i], device_id=other, device_id_type=BY_MESH
        )

    center = slice(4 * ATOMS, 5 * ATOMS)
    asks = [far(ask, ask_in, 0), far(places.at[:, center], pos_in, 1)]
    for copy in asks:
        copy.start()
    spot_copies, copies = [], []
    for i, (da, db) in enumerate(PLANES):
        place = (1 - da) * 3 + (1 - db)
        span = slice(place * ATOMS, (place + 1) * ATOMS)
        for group, source, target, s, r in (
            (spot_copies, places.at[:, center], places.at[:, span], pos_send, pos_recv),
            (copies, mine, table.at[:, span], send, recv),
        ):
            group.append(
                pltpu.make_async_remote_copy(
                    source, target, s.at[i], r.at[i], device_id=plane(da, db), device_id_type=BY_MESH
                )
            )
    for copy in spot_copies + copies:
        copy.start()
    scalars_far = far(mine.at[:CHAN], own_in, 2)
    scalars_far.start()
    points_far = far(points, points_in, 3)
    points_far.start()

    shift_own = fill_pick(pick_own, ask[:NEIGH], ask[NEIGH : NEIGH + 1], True)
    fill_cells(spots_own, cells)
    for copy in asks + spot_copies:
        copy.wait_recv()
    shift_par = fill_pick(pick_par, ask_in[:NEIGH], ask_in[NEIGH : NEIGH + 1], False)
    fill_radial(
        radial_par, units_par, pick_par, places, shift_par, pos_in[...].astype(F32), rin, rout
    )
    fill_radial(radial_own, units_own, pick_own, places, shift_own, pos_pad[...], rin, rout)
    for copy in copies:
        copy.wait_recv()
    sums = edge_sums(table, pick_par, radial_par, units_par)
    for i in range(4):
        part[i * CHAN : (i + 1) * CHAN, :] = sums[i].astype(BF16)
    partial = far(part, part_in, 4)
    partial.start()
    sums = edge_sums(table, pick_own, radial_own, units_own)
    same[...] = sums[0].astype(BF16)
    same_far = far(same, same_in, 5)
    same_far.start()
    points_far.wait_recv()
    for d in range(3):
        cells_par[d] = points_in[d].astype(F32).astype(I32)
    fill_cells(spots_par, cells_par)

    kz = c * 128 + b * 16 + a // 2
    ky = lax.rem(a, 2) * 128 + lax.broadcasted_iota(I32, (MESH, 128), 1)
    kx = lax.broadcasted_iota(I32, (MESH, 128), 0)
    fz = jnp.where(kz <= 128, kz, kz - 128).astype(F32)
    step_size = 2.0 * math.pi / MESH
    screen = 4.0 * math.pi / MESH
    fx, fy = signed(kx), signed(ky)
    ksquare = step_size * step_size * (fx * fx + fy * fy + fz * fz)
    green = jnp.exp(-0.5 * ksquare) / (ksquare + screen * screen)
    green = jnp.where((kx + ky + kz) == 0, 0.0, green)

    scalars_far.wait_recv()
    same_far.wait_recv()
    partial.wait_recv()

    def gather_sum(layer, far_part):
        return ((layer.astype(F32) + far_part.astype(F32)) / NEIGH).astype(BF16)

    head_row = head[...]

    def charge_of(scalars):
        high, low = halves_of(head_row)
        rows = jnp.concatenate([high, low, low - low.astype(BF16).astype(F32)], axis=0)
        return jnp.sum(dot_nn(rows.astype(BF16), scalars), axis=0, keepdims=True)

    agg_s = gather_sum(same[...], part_in[:CHAN, :])
    agg_par = gather_sum(same_in[...], part[:CHAN, :])
    scalars = (own[:CHAN] + silu(dot_tn(mix_s[...], agg_s))).astype(BF16)
    scalars_par = (
        own_in[...].astype(F32) + silu(dot_tn(mix_s[...], agg_par))
    ).astype(BF16)
    charge = charge_of(scalars)
    charge_par = charge_of(scalars_par)

    value[...] = weight[...] * charge
    spread(density_own, spots_own, cells, value)
    value[...] = points_in[3].astype(F32) * charge_par
    spread(density_par, spots_par, cells_par, value)
    fwd_own, fwd_par = z_fwd[c, c], z_fwd[c, 1 - c]
    for g in range(5):
        span = slice(g * 128, (g + 1) * 128)
        modes[g, :, :] = (
            dot_nt(fwd_own, density_own[span, :].astype(BF16))
            + dot_nt(fwd_par, density_par[span, :].astype(BF16))
        ).astype(BF16)

    def grid_tile(ref):
        return lambda i: ref.at[tile(i // 2, 16), tile(lax.rem(i, 2), 128)]

    def row_tile(ref):
        return lambda i: ref.at[tile(i, 16), :]

    def mid_tile(ref):
        return lambda i: ref.at[:, tile(i, 16), :]

    def lane_tile(ref):
        return lambda i: ref.at[:, :, tile(i, 128)]

    first = Exchange(GY, b, mid_tile(modes), lane_tile(in1), send1, recv1, gy_id)
    second = Exchange(GX, a, grid_tile(out2), row_tile(in2), send2, recv2, gx_id)
    third = Exchange(GX, a, row_tile(out3), grid_tile(in3), send3, recv3, gx_id)
    fourth = Exchange(GY, b, lane_tile(out4), mid_tile(in4), send4, recv4, gy_id)

    first.run()
    mixed = dot_nn(in1[...].reshape(80, 1024), y_mat[...])
    stacked = jnp.concatenate(
        [mixed[:, i * MESH : (i + 1) * MESH].astype(BF16) for i in range(3)], axis=0
    )
    out2[...] = dot_nn(order[...], stacked).astype(BF16)
    second.run()
    spectrum = dot_nn(x_fwd[...], in2[...]) * green
    out3[...] = dot_nn(x_inv[...], spectrum.astype(BF16)).astype(BF16)
    third.run()
    stacked = dot_nn(back[...], in3[...]).astype(BF16)
    joined = jnp.concatenate([stacked[80 * i : 80 * (i + 1)] for i in range(3)], axis=1)
    out4[...] = dot_nt(joined, y_mat[...]).astype(BF16).reshape(5, 16, 1024)
    fourth.run()

    def potential(matrix):
        for g in range(5):
            field[:, g * 128 : (g + 1) * 128] = dot_nn(matrix, in4[g]).astype(BF16)

    potential(z_inv[c, 1 - c])
    collect(values, spots_par, cells_par, field)
    found = values[...]
    for d in range(3):
        force[d : d + 1, :] = jnp.sum(
            points_in[4 + d].astype(F32) * found, axis=0, keepdims=True
        )
    force[3:, :] = jnp.zeros((5, ATOMS), F32)
    forces_far = far(force, force_in, 6)
    forces_far.start()
    potential(z_inv[c, c])
    collect(values, spots_own, cells, field)
    found = values[...]
    totals = [jnp.sum(slope[d] * found, axis=0, keepdims=True) for d in range(3)]

    agg_v = [
        gather_sum(sums[d + 1], part_in[(d + 1) * CHAN : (d + 2) * CHAN, :]) for d in range(3)
    ]
    gate = 1.0 / (1.0 + jnp.exp(-dot_tn(mix_g[...], agg_s)))
    vectors = [
        own[CHAN * (d + 1) : CHAN * (d + 2)] + dot_tn(mix_v[...], agg_v[d]) * gate
        for d in range(3)
    ]
    result = jnp.concatenate([scalars.astype(F32)] + vectors, axis=0)
    updated[...] = result.T.astype(BF16)
    for copy in asks + spot_copies + copies + [scalars_far, points_far, partial, same_far]:
        copy.wait_send()
    for step in (first, second, third, fourth):
        step.finish()
    forces_far.wait()
    for d in range(3):
        forces[d] = -charge * (totals[d] + force_in[d : d + 1, :])


LIMIT = 60 * 1024 * 1024
DMA = pltpu.SemaphoreType.DMA


def per_device(
    features, positions, neighbours, counts, cell_index, spline_weight, spline_slope,
    radial_in, radial_out, mix_scalar, mix_vector, mix_gate, charge_head,
):
    consts = tables()
    inputs = [
        features[0, 0, 0], positions[0, 0, 0], neighbours.reshape(NEIGH, 1, ATOMS), counts[0, 0],
        cell_index[0, 0, 0], spline_weight[0, 0, 0], spline_slope[0, 0, 0],
        radial_in, radial_out, mix_scalar, mix_vector, mix_gate, charge_head[None, :],
    ] + consts
    fetched = [inputs[i] for i in (0, 2, 4, 5, 6, 7, 8, 9, 10, 11)] + consts
    edges = NEIGH * ATOMS
    buffer = lambda shape, dtype: pltpu.VMEM(shape, dtype)
    updated, forces = pl.pallas_call(
        whole_kernel,
        out_shape=(
            jax.ShapeDtypeStruct((ATOMS, 4 * CHAN), BF16),
            jax.ShapeDtypeStruct((3, 1, ATOMS), F32),
        ),
        in_specs=[ANY, VMEM, ANY, VMEM] + [ANY] * 8 + [VMEM] + [ANY] * 7,
        out_specs=(VMEM, VMEM),
        scratch_shapes=[buffer(x.shape, x.dtype) for x in fetched]
        + [
            DMA((17,)),
            buffer((256, ATOMS), BF16),
            buffer((256, 9 * ATOMS), BF16),
            buffer((16, 9 * ATOMS), BF16),
            buffer((16, ATOMS), F32),
            buffer((16, ATOMS), I32),
            buffer((16, ATOMS), I32),
            buffer((16, ATOMS), BF16),
            buffer((CHAN, ATOMS), BF16),
            buffer((256, ATOMS), BF16),
            buffer((256, ATOMS), BF16),
            buffer((CHAN, ATOMS), BF16),
            buffer((CHAN, ATOMS), BF16),
            buffer((7, SPLINE, ATOMS), BF16),
            buffer((7, SPLINE, ATOMS), BF16),
            buffer((3, SPLINE, ATOMS), I32),
            buffer((9 * ATOMS, edges), BF16),
            buffer((9 * ATOMS, edges), BF16),
            buffer((3 * CHAN, edges), F32),
            buffer((3 * CHAN, edges), F32),
            buffer((8, edges), F32),
            buffer((8, edges), F32),
            buffer((CHUNKS, ROWS, WIDTH), BF16),
            buffer((CHUNKS, ROWS, WIDTH), BF16),
            buffer((SPLINE, ATOMS), F32),
            buffer((ROWS, ZPAD), F32),
            buffer((ROWS, ZPAD), F32),
            buffer((5, 128, 128), BF16),
            buffer((5, 16, 1024), BF16),
            buffer((256, 256), BF16),
            buffer((512, 128), BF16),
            buffer((512, 128), BF16),
            buffer((256, 256), BF16),
            buffer((5, 16, 1024), BF16),
            buffer((5, 128, 128), BF16),
            buffer((ZPAD, ROWS), BF16),
            buffer((SPLINE, ATOMS), F32),
            buffer((8, ATOMS), F32),
            buffer((8, ATOMS), F32),
            DMA((8,)), DMA((8,)), DMA((8,)), DMA((8,)), DMA((7,)), DMA((7,)),
            DMA((GY,)), DMA((GY,)), DMA((GX,)), DMA((GX,)),
            DMA((GX,)), DMA((GX,)), DMA((GY,)), DMA((GY,)),
        ],
        compiler_params=pltpu.CompilerParams(
            collective_id=0, has_side_effects=True, vmem_limit_bytes=LIMIT
        ),
        name="whole",
    )(*inputs)
    return (updated[None, None, None], forces.reshape(1, 1, 1, 3, ATOMS))


def solution(mesh):
    placed = (
        P("gx", "gy", "gz", None, None),
        P("gx", "gy", "gz", None, None),
        P("gx", "gy", "gz", None, None),
        P("gx", "gy", "gz", None),
        P("gx", "gy", "gz", None, None, None),
        P("gx", "gy", "gz", None, None),
        P("gx", "gy", "gz", None, None, None),
        P(), P(), P(), P(), P(), P(),
    )
    return jax.shard_map(
        per_device,
        mesh=mesh,
        in_specs=placed,
        out_specs=(P("gx", "gy", "gz", None, None), P("gx", "gy", "gz", None, None)),
        check_vma=False,
    )
```

time: 133 us -> 103 us (0.77)
  Pallas kernels: 116 us -> 98.9 us
  local copies, waits for them, and re-layouts: 14.8 us -> 2.7 us
    pallas_call x4 -> x1, Pallas kernels: 116 us -> 98.9 us  [per_device(): pl.pallas_call(whole_kernel, out_shape=(jax.ShapeDtypeStruct((ATOMS, 4 *...]
    unnamed x34 -> x2, local copies, waits for them, and re-layouts: 14.1 us -> 2.7 us
where the time goes in v2:
time: 103 us; the launch traced here: 102 us
  Pallas kernels  98.9 us (96%)
  local copies, waits for them, and re-layouts  2.7 us (3%)
    pallas_call x1, Pallas kernels, per_device(): pl.pallas_call(whole_kernel, out_shape=(jax.ShapeDtypeStruct((ATOMS, 4 *...  98.9 us
    unnamed x2, local copies, waits for them, and re-layouts  2.7 us

profile of v2, /device:TPU:1, one launch (start us, length us, event | category | flops | bytes accessed | tf_op | source)
XLA Modules:
  0.0 102.3 jit_solution(17349323096461403807)
XLA Ops:
  0.6 98.9 %whole.1 = (bf16[128,256]{1,0:T(8,128)(2,1)}, f32[3,1,128]{2,1,0:T(1,128)}) custom-call(bf16[128,256]{1,0:T(8,128)(2,1)} %bitcast.14, bf16[3,128]{1,0:T(4,128)(2,1)} %bitcast.19, s32[12,1,128]{2,1,0:T(1,128)} %bitcast.17, s32[1,128]{1,0:T(1,128)} %bitcast.20, s32[3,64,128]{2,1,0:T(8,128)} %bitcast.12, f32[64,128]{1,0:T(8,128)} %bitcast.16, ...), custom_call_target="tpu_custom_call" | custom-call | tf_op jit(solution)/shard_map/whole/pallas_call | solution.py:529
  99.6 1.5 %copy.25 = bf16[1,1,1,128,256]{4,3,2,1,0:T(8,128)(2,1)} copy(bf16[1,1,1,128,256]{4,3,2,1,0:T(8,128)(2,1)} %bitcast.15) | data formatting | bytes 131072
  101.1 1.2 %copy.26 = f32[1,1,1,3,128]{4,2,3,1,0:T(1,128)} copy(f32[1,1,1,3,128]{4,2,3,1,0:T(1,128)} %bitcast.18) | data formatting | bytes 3072
